TPU v7x, 512 devices: a whole 4x4x16 slice. The times are simulated.
512 devices in a mesh: pts: 128 (over z, x, core), head: 4 (over y).
Axes of the slice: x: 4, y: 4, z: 16, core: 2. Of those that a mesh axis runs over, the one named last changes fastest.
Arguments:
- query_pool: bfloat16 [73728, 768], P('pts', 'head'), may hold values from -24 to 24
- sample_index: int32 [36864], P('pts'), may hold values from 0 to 575
- labels: int32 [36864], P('pts'), may hold values 0 or 1
- w_query: bfloat16 [768, 768], P(None, 'head'), may hold values from -0.21875 to 0.21875
- keys: bfloat16 [1024, 768], P('pts', 'head'), may hold values from -121.5 to 121.5
- values: bfloat16 [1024, 768], P('pts', 'head'), may hold values from -6 to 6
- w_out: bfloat16 [768, 768], P('head'), may hold values from -0.21875 to 0.21875
- out_gain: bfloat16 [768], replicated, may hold values from 0.099609375 to 1.8984375
- w_hidden: bfloat16 [768, 1536], P(None, 'head'), may hold values from -0.21875 to 0.21875
- w_logit: bfloat16 [1536], P('head'), may hold values from -0.15625 to 0.15625
Outputs:
- grad_query_weight: float32 [768, 768], P(None, 'head')
- grad_out_weight: float32 [768, 768], P('head')
- grad_hidden_weight: float32 [768, 1536], P(None, 'head')
- grad_logit_weight: float32 [1536], P('head')
- grad_gain: float32 [768], replicated
- grad_keys: float32 [1024, 768], P('pts', 'head')
- grad_values: float32 [1024, 768], P('pts', 'head')
Inputs may be any that keep to these rules, and one draw needn't show every extreme that they name: `sample_index`: each entry names a row of the block of 576 candidate rows that holds its point's block, counted from that block's start.
All inputs are finite; a program needn't handle non-finite values. No bound on the sum of `labels` on one device may be relied on, other than what follows from the above.
Results may differ from a plain program's by a relative error of at most 0.03.
Values may be sent and summed in bfloat16 or wider, within the bound.
A program may use at most 64 MiB of HBM per device.

v0:
```python
import jax
import jax.numpy as jnp
from jax import lax
from jax.sharding import PartitionSpec as P

HD = 64


EPSILON = 1e-05


def on_device(
    query_pool, sample_index, labels, w_query, keys, values, w_out, out_gain, w_hidden, w_logit
):
    scale = HD ** (-0.5)
    picked = jnp.take(query_pool, sample_index, axis=0)
    rows_in = lax.all_gather(picked, "head", axis=1, tiled=True)
    full_keys, full_values = (
        lax.all_gather(keys, "pts", axis=0, tiled=True),
        lax.all_gather(values, "pts", axis=0, tiled=True),
    )
    points = rows_in.shape[0]
    latent_count = full_keys.shape[0]
    local_heads = w_query.shape[1] // HD
    gain = out_gain.astype(jnp.float32)
    query = jnp.dot(rows_in, w_query, preferred_element_type=jnp.float32).astype(jnp.bfloat16)
    query_heads = query.reshape(points, local_heads, HD)
    key_heads = full_keys.reshape(latent_count, local_heads, HD)
    value_heads = full_values.reshape(latent_count, local_heads, HD)
    scores = (
        jnp.einsum("phd,lhd->hpl", query_heads, key_heads, preferred_element_type=jnp.float32)
        * scale
    )
    probs = jax.nn.softmax(scores, axis=-1).astype(jnp.bfloat16)
    att_heads = jnp.einsum(
        "hpl,lhd->phd", probs, value_heads, preferred_element_type=jnp.float32
    ).astype(jnp.bfloat16)
    attended = att_heads.reshape(points, -1)
    partial_out = jnp.dot(attended, w_out, preferred_element_type=jnp.float32)
    mixed = rows_in.astype(jnp.float32) + lax.psum(partial_out, "head")
    mean = jnp.mean(mixed, axis=-1, keepdims=True)
    center = mixed - mean
    var = jnp.mean(center * center, axis=-1, keepdims=True)
    rstd = lax.rsqrt(var + EPSILON)
    normal_rows = center * rstd
    normed = (normal_rows * gain).astype(jnp.bfloat16)
    hidden_pre = jnp.dot(normed, w_hidden, preferred_element_type=jnp.float32)
    activated = jax.nn.gelu(hidden_pre).astype(jnp.bfloat16)
    logit = lax.psum(jnp.dot(activated, w_logit, preferred_element_type=jnp.float32), "head")
    total_points = points * lax.axis_size("pts")
    d_logit = (jax.nn.sigmoid(logit) - labels.astype(jnp.float32)) * total_points ** (-0.5)
    grad_w2 = jnp.dot(d_logit, activated.astype(jnp.float32))
    _, pull = jax.vjp(jax.nn.gelu, hidden_pre)
    d_hidden = pull(d_logit[:, None] * w_logit.astype(jnp.float32)[None, :])[0].astype(jnp.bfloat16)
    grad_w1 = jnp.einsum("pd,pf->df", normed, d_hidden, preferred_element_type=jnp.float32)
    d_normed_part = jnp.einsum("pf,df->pd", d_hidden, w_hidden, preferred_element_type=jnp.float32)
    d_normed = lax.psum(d_normed_part, "head")
    grad_g = jnp.sum(d_normed * normal_rows, axis=0)
    scaled = d_normed * gain
    d_mixed = rstd * (
        scaled
        - jnp.mean(scaled, axis=-1, keepdims=True)
        - normal_rows * jnp.mean(scaled * normal_rows, axis=-1, keepdims=True)
    )
    d_mixed = d_mixed.astype(jnp.bfloat16)
    grad_wo = jnp.einsum("pc,pd->cd", attended, d_mixed, preferred_element_type=jnp.float32)
    d_attended = jnp.einsum("pd,cd->pc", d_mixed, w_out, preferred_element_type=jnp.float32).astype(
        jnp.bfloat16
    )
    d_att_heads = d_attended.reshape(points, local_heads, HD)
    d_probs = jnp.einsum(
        "phd,lhd->hpl", d_att_heads, value_heads, preferred_element_type=jnp.float32
    )
    delta = jnp.einsum(
        "phd,phd->hp", d_att_heads.astype(jnp.float32), att_heads.astype(jnp.float32)
    )
    d_scores = (probs.astype(jnp.float32) * (d_probs - delta[:, :, None]) * scale).astype(
        jnp.bfloat16
    )
    d_query = jnp.einsum("hpl,lhd->phd", d_scores, key_heads, preferred_element_type=jnp.float32)
    d_query = d_query.astype(jnp.bfloat16).reshape(points, -1)
    grad_wq = jnp.einsum("pd,pc->dc", rows_in, d_query, preferred_element_type=jnp.float32)
    count = lax.axis_size("pts") * keys.shape[0]
    key_part = jnp.einsum("hpl,phd->lhd", d_scores, query_heads, preferred_element_type=jnp.float32)
    value_part = jnp.einsum("hpl,phd->lhd", probs, d_att_heads, preferred_element_type=jnp.float32)
    latent_grads = lax.psum_scatter(
        jnp.concatenate([key_part.reshape(count, -1), value_part.reshape(count, -1)], axis=1),
        "pts",
        scatter_dimension=0,
        tiled=True,
    )
    columns = keys.shape[1]
    grad_k = latent_grads[:, :columns]
    grad_v = latent_grads[:, columns:]
    out_wq, out_wo, out_w1, summed_w2, summed_g = lax.psum(
        (grad_wq, grad_wo, grad_w1, grad_w2, grad_g), "pts"
    )
    return (out_wq, out_wo, out_w1, summed_w2, summed_g, grad_k, grad_v)


def solution(mesh):
    return jax.shard_map(
        on_device,
        mesh=mesh,
        in_specs=(
            P("pts", "head"),
            P("pts"),
            P("pts"),
            P(None, "head"),
            P("pts", "head"),
            P("pts", "head"),
            P("head", None),
            P(),
            P(None, "head"),
            P("head"),
        ),
        out_specs=(
            P(None, "head"),
            P("head", None),
            P(None, "head"),
            P("head"),
            P(),
            P("pts", "head"),
            P("pts", "head"),
        ),
        check_vma=False,
    )
```

profile of v0, /device:TPU:1, one launch (start us, length us, event | category | flops | bytes accessed | tf_op | source)
XLA Modules:
  0.0 722.0 jit_solution(13755983757687087459)
XLA Ops:
  9.8 2.0 gather_fusion
  12.1 11.5 %all_gather.9 = bf16[288,768]{0,1:T(8,128)(2,1)S(1)} all-gather(bf16[288,192]{0,1:T(8,128)(2,1)S(1)} %copy.23), channel_id=1, replica_groups=mesh['pts'=128,'head'=4] {'head'}, dimensions={1}, use_global_device_ids=true | all-gather | bytes 552960 | tf_op jit(solution)/shard_map/all_gather | solution.py:17
  23.6 93.0 %all_gather.10 = bf16[1024,192]{1,0:T(8,128)(2,1)S(1)} all-gather(bf16[8,192]{1,0:T(8,128)(2,1)S(1)} %copy-done.16), channel_id=1, replica_groups=mesh['pts'=128,'head'=4] {'pts'}, dimensions={0}, use_global_device_ids=true | all-gather | bytes 396288 | tf_op jit(solution)/shard_map/all_gather | solution.py:19
  116.8 81.9 %all_gather.11 = bf16[1024,192]{1,0:T(8,128)(2,1)S(1)} all-gather(bf16[8,192]{1,0:T(8,128)(2,1)S(1)} %copy-done.17), channel_id=1, replica_groups=mesh['pts'=128,'head'=4] {'pts'}, dimensions={0}, use_global_device_ids=true | all-gather | bytes 396288 | tf_op jit(solution)/shard_map/all_gather | solution.py:20
  199.3 3.0 fusion.27
  202.3 2.4 divide_convert_fusion
  205.7 1.2 fusion.28
  208.0 52.5 %all-reduce.7.cloned.1.call-done = f32[288,768]{1,0:T(8,128)} async-done(((f32[288,768]{1,0:T(8,128)}), f32[288,768]{1,0:T(8,128)}) %all-reduce.7.cloned.1.call-update) | async-done | bytes 884752 | tf_op jit(solution)/shard_map/psum | solution.py:40
  260.5 1.5 fusion.25
  262.3 1.2 multiply_convert_fusion.3
  264.4 8.0 %psum.57 = f32[288]{0:T(512)S(1)} all-reduce(f32[288]{0:T(512)S(1)} %convolution_reduce_fusion.1), channel_id=1, replica_groups=mesh['pts'=128,'head'=4] {'head'}, use_global_device_ids=true, to_apply=%region_5.6 | all-reduce | flops 288 | bytes 2304 | tf_op jit(solution)/shard_map/psum | solution.py:49
  272.3 2.6 fusion.23
  275.0 2.9 fusion.20
  277.9 58.7 %all-reduce.9.cloned.1.call-done = f32[288,768]{1,0:T(8,128)} async-done(((f32[288,768]{1,0:T(8,128)}), f32[288,768]{1,0:T(8,128)}) %all-reduce.9.cloned.1.call-update) | async-done | bytes 884752 | tf_op jit(solution)/shard_map/psum | solution.py:57
  336.6 1.7 multiply_reduce_fusion.1
  343.0 1.4 fusion.31
  345.9 1.5 copy.27
  347.4 1.5 pad_maximum_fusion
  348.9 1.3 dynamic-slice
  351.1 254.7 %all-reduce.1 = (f32[384]{0:T(512)}, f32[768]{0:T(1024)}) all-reduce(f32[384]{0:T(512)S(1)} %convolution_reduce_fusion, f32[768]{0:T(1024)S(1)} %get-tuple-element.7), channel_id=1, replica_groups=mesh['pts'=128,'head'=4] {'pts'}, use_global_device_ids=true, to_apply=%region_12.13 | all-reduce | flops 1152 | bytes 9216 | tf_op jit(solution)/shard_map/psum | solution.py:95
  605.8 103.3 %all-reduce.11.cloned.1.call-done = (f32[768,192]{0,1:T(8,128)}, f32[192,768]{1,0:T(8,128)}, f32[768,384]{1,0:T(8,128)}, f32[1024,384]{1,0:T(8,128)}) async-done(((f32[768,192]{0,1:T(8,128)}, f32[192,768]{1,0:T(8,128)}, f32[768,384]{1,0:T(8,128)}, f32[1024,384]{1,0:T(8,128)}), (f32[768,192]{0,1:T(8,128)}, f32[192,768]{1,0:T(8,128)}, f32[768,384]{1,0:T(8,128)}, ...) | async-done | bytes 3932176 | tf_op jit(solution)/shard_map/psum | solution.py:95
  709.1 1.5 fusion.26
  710.6 1.9 copy.42
  712.5 1.9 copy.43
  (80 shorter events, 14.1 us)
Async XLA Ops:
  7.2 255.1 %copy-start = (bf16[768,384]{1,0:T(8,128)(2,1)S(1)}, bf16[768,384]{1,0:T(8,128)(2,1)}, u32[]{:S(2)}) copy-start(bf16[768,384]{1,0:T(8,128)(2,1)} %param.18) | copy-start | bytes 1769476
  7.2 16.4 %copy-start.16 = (bf16[8,192]{1,0:T(8,128)(2,1)S(1)}, bf16[8,192]{1,0:T(8,128)(2,1)}, u32[]{:S(2)}) copy-start(bf16[8,192]{1,0:T(8,128)(2,1)} %param.14) | copy-start | bytes 9220
  7.2 253.3 %all-reduce.7.cloned.1.call-start = ((), (), s32[]{:S(2)}) async-start(), calls=%async_computation | async-start | bytes 1769472 | tf_op jit(solution)/shard_map/psum | solution.py:40
  9.8 107.0 %copy-start.17 = (bf16[8,192]{1,0:T(8,128)(2,1)S(1)}, bf16[8,192]{1,0:T(8,128)(2,1)}, u32[]{:S(2)}) copy-start(bf16[8,192]{1,0:T(8,128)(2,1)} %param.15) | copy-start | bytes 9220
  12.0 186.9 %copy-start.15 = (bf16[768,192]{0,1:T(8,128)(2,1)S(1)}, bf16[768,192]{0,1:T(8,128)(2,1)}, u32[]{:S(2)}) copy-start(bf16[768,192]{0,1:T(8,128)(2,1)} %param.13) | copy-start | bytes 884740
  23.6 183.4 %copy-start.1 = (bf16[288,768]{0,1:T(8,128)(2,1)}, bf16[288,768]{0,1:T(8,128)(2,1)S(1)}, u32[]{:S(2)}) copy-start(bf16[288,768]{0,1:T(8,128)(2,1)S(1)} %all_gather.9) | copy-start | bytes 1327108
  116.8 85.5 %copy-start.4 = (bf16[1024,192]{0,1:T(8,128)(2,1)}, bf16[1024,192]{0,1:T(8,128)(2,1)S(1)}, u32[]{:S(2)}) copy-start(bf16[1024,192]{0,1:T(8,128)(2,1)S(1)} %copy.24) | copy-start | bytes 1179652
  198.9 5.8 copy-start.6
  199.3 3.0 copy-start.13
  204.7 1.0 copy-start.9
  204.7 2.2 copy-start.18
  205.4 2.6 copy-start.19
  206.9 129.7 %all-reduce.9.cloned.1.call-start = ((), (), s32[]{:S(2)}) async-start(), calls=%async_computation.1 | async-start | bytes 1769472 | tf_op jit(solution)/shard_map/psum | solution.py:57
  262.0 10.4 %copy-start.20 = (s32[288]{0:T(512)S(1)}, s32[288]{0:T(512)}, u32[]{:S(2)}) copy-start(s32[288]{0:T(512)} %param.12) | copy-start | bytes 3460
  263.5 0.7 copy-start.11
  275.0 434.2 %all-reduce.11.cloned.1.call-start = ((), (), s32[]{:S(2)}) async-start(), calls=%async_computation.2 | async-start | bytes 7864320 | tf_op jit(solution)/shard_map/psum | solution.py:95
  336.6 1.7 copy-start.3
  336.6 2.0 copy-start.10
  340.1 1.0 copy-start.7
  341.1 1.0 copy-start.5
  342.1 0.9 copy-start.14
  343.0 1.4 copy-start.2
  348.9 2.0 copy-start.12
  709.1 5.3 copy-start.8
Sparse Core Ops, SparseCore 0:
  207.0 53.4 all-reduce.6
  275.1 61.5 all-reduce.8
  349.1 360.0 all-reduce.10
where the time goes:
time: 723 us; the launch traced here: 722 us
  blocking collectives  449 us (62%)
  waiting for transfers between devices  215 us (30%)
  matrix products  18.3 us (3%)
  local copies, waits for them, and re-layouts  15.9 us (2%)
  between operations  14.7 us (2%)
  other arithmetic  9.25 us (1%)
    psum x1, blocking collectives, on_device(): lax.psum((grad_wq, grad_wo, grad_w1, grad_w2, grad_g), 'pts')  255 us
    psum x1, waiting for transfers between devices, on_device(): lax.psum((grad_wq, grad_wo, grad_w1, grad_w2, grad_g), 'pts')  103 us
    all_gather x1, blocking collectives, on_device(): lax.all_gather(keys, 'pts', axis=0, tiled=True)  93 us
    all_gather x1, blocking collectives, on_device(): lax.all_gather(values, 'pts', axis=0, tiled=True)  81.9 us
    psum x1, waiting for transfers between devices, on_device(): d_normed = lax.psum(d_normed_part, 'head')  58.7 us
    psum x1, waiting for transfers between devices, on_device(): mixed = rows_in.astype(jnp.float32) + lax.psum(partial_out, 'head')  52.5 us
  transfers between devices with their start and end apart: 3, of which 3 were waited for; matrix products, arithmetic and copies ran while one was open for 1% of the time, Pallas kernels for 0%

commit v1 on v0

v1 whole, which is shorter than its diff:
```python
import jax
import jax.numpy as jnp
from jax import lax
from jax.experimental import pallas as pl
from jax.experimental.pallas import tpu as pltpu
from jax.sharding import PartitionSpec as P

HD = 64
EPSILON = 1e-05
NX = 4
NC = 2
PIECES = 9
MESH = pl.DeviceIdType.MESH
F32 = jnp.float32
BF16 = jnp.bfloat16


def dot(a, b):
    return jnp.dot(a, b, preferred_element_type=F32)


def dot_nt(a, b):
    return lax.dot_general(a, b, (((1,), (1,)), ((), ())), preferred_element_type=F32)


class Links:
    def __init__(self, nz, ny, sems):
        self.nz, self.ny, self.sems, self.used = nz, ny, sems, 0
        p = lax.axis_index("pts")
        self.y = lax.axis_index("head")
        self.c = p % NC
        self.x = (p // NC) % NX
        self.z = p // (NC * NX)
        self.other = 1 - self.c
        self.ends = []

    def at(self, x=None, y=None, z=None, c=None):
        x = self.x if x is None else x
        y = self.y if y is None else y
        z = self.z if z is None else z
        c = self.c if c is None else c
        return (z * (NC * NX) + x * NC + c, y)

    def x_at(self, d):
        return self.at(x=(self.x + d) % NX)

    def y_at(self, d):
        return self.at(y=(self.y + d) % self.ny)

    def z_at(self, d):
        return self.at(z=(self.z + d) % self.nz)

    def sibling(self):
        return self.at(c=self.other)

    def take(self, count):
        first = self.used
        self.used += count
        return first

    def copy(self, src, dst, send, recv, device):
        return pltpu.make_async_remote_copy(
            src_ref=src,
            dst_ref=dst,
            send_sem=self.sems.at[send],
            recv_sem=self.sems.at[recv],
            device_id=device,
            device_id_type=MESH,
        )

    def send(self, src, dst, send, recv, device):
        copy = self.copy(src, dst, send, recv, device)
        copy.start()
        self.ends.append(copy.wait_send)

    def arrived(self, dst, recv):
        self.copy(dst, dst, recv, recv, self.sibling()).wait_recv()

    def finish(self):
        for end in self.ends:
            end()


class WeightSum:
    def __init__(self, net, refs, mirrored):
        self.net, self.mirrored = net, mirrored
        self.part, self.cr, self.xs, self.xr, self.zs, self.zr, self.full = refs
        nz = net.nz
        self.s_core, self.r_core = net.take(1), net.take(1)
        self.s_x, self.r_x = net.take(NX - 1), net.take(NX - 1)
        self.s_z, self.r_z = net.take(PIECES), net.take(nz - 1)
        self.s_gz, self.r_gz = net.take(nz - 1), net.take(PIECES)
        self.s_gx, self.r_gx = net.take(NX - 1), net.take(NX - 1)
        self.s_gc, self.r_gc = net.take(1), net.take(1)
        mine = (nz - 1 - net.z) if mirrored else net.z
        self.piece = (PIECES * mine + nz - 1) // nz
        self.reduces = (nz * self.piece) // PIECES == mine

    def owner(self, piece):
        spot = (self.net.nz * piece) // PIECES
        return self.net.nz - 1 - spot if self.mirrored else spot

    def put(self, c, x, block):
        block = block.astype(BF16)
        for j in range(PIECES):
            r, l = 16 * (j // 3), 128 * (j % 3)
            self.part[c, x, j] = block[r : r + 16, l : l + 128]

    def start(self):
        net = self.net
        net.send(self.part.at[net.other], self.cr, self.s_core, self.r_core, net.sibling())

    def to_x(self):
        net = self.net
        net.arrived(self.cr, self.r_core)
        self.xs[...] = (self.part[net.c].astype(F32) + self.cr[...].astype(F32)).astype(BF16)
        for d in range(1, NX):
            target = (net.x + d) % NX
            net.send(
                self.xs.at[target], self.xr.at[d - 1], self.s_x + d - 1, self.r_x + d - 1, net.x_at(d)
            )

    def to_z(self):
        net = self.net
        total = self.xs[net.x].astype(F32)
        for d in range(1, NX):
            net.arrived(self.xr.at[d - 1], self.r_x + d - 1)
            total += self.xr[d - 1].astype(F32)
        self.zs[...] = total.astype(BF16)
        for j in range(PIECES):
            way = (self.owner(j) - net.z + net.nz) % net.nz

            def copy(j=j, way=way):
                return net.copy(
                    self.zs.at[j],
                    self.zr.at[way - 1],
                    self.s_z + j,
                    self.r_z + way - 1,
                    net.at(z=self.owner(j)),
                )

            @pl.when(way != 0)
            def _(copy=copy):
                copy().start()

            @net.ends.append
            def _(copy=copy, way=way):
                @pl.when(way != 0)
                def _():
                    copy().wait_send()

    def back_z(self):
        net = self.net
        tile = self.full.at[net.c, net.x, self.piece]

        def copy(d):
            return net.copy(tile, tile, self.s_gz + d - 1, self.r_gz + self.piece, net.z_at(d))

        @pl.when(self.reduces)
        def _():
            total = self.zs[self.piece].astype(F32)
            for d in range(1, net.nz):
                net.arrived(self.zr.at[d - 1], self.r_z + d - 1)
                total += self.zr[d - 1].astype(F32)
            self.full[net.c, net.x, self.piece] = total.astype(BF16)
            for d in range(1, net.nz):
                copy(d).start()

        @net.ends.append
        def _():
            @pl.when(self.reduces)
            def _():
                for d in range(1, net.nz):
                    copy(d).wait_send()

    def back_x(self):
        net = self.net
        for j in range(PIECES):

            @pl.when(net.z != self.owner(j))
            def _(j=j):
                net.arrived(self.full.at[net.c, net.x, j], self.r_gz + j)

        mine = self.full.at[net.c, net.x]
        for d in range(1, NX):
            net.send(mine, mine, self.s_gx + d - 1, self.r_gx + d - 1, net.x_at(d))

    def back_core(self):
        net = self.net
        for d in range(1, NX):
            source = (net.x + NX - d) % NX
            net.arrived(self.full.at[net.c, source], self.r_gx + d - 1)
        mine = self.full.at[net.c]
        net.send(mine, mine, self.s_gc, self.r_gc, net.sibling())

    def end(self):
        net = self.net
        net.arrived(self.full.at[net.other], self.r_gc)

    def block(self, c, x):
        rows = []
        for r in range(3):
            rows.append(jnp.concatenate([self.full[c, x, 3 * r + l] for l in range(3)], axis=1))
        return jnp.concatenate(rows, axis=0)


def kernel(
    nz,
    ny,
    pool_ref,
    index_ref,
    label_ref,
    w_query_ref,
    kv_ref,
    w_out_ref,
    gain_ref,
    w_hidden_ref,
    w_logit_ref,
    owh_ref,
    owo_ref,
    owq_ref,
    small_ref,
    okv_ref,
    rows_buf,
    rows_in,
    wo_full,
    wh_full,
    wl_full,
    kvx,
    kv_buf,
    q_ref,
    probs,
    att_t,
    att_buf,
    normal_ref,
    normed_ref,
    act_ref,
    slope_ref,
    dh_ref,
    ws_part,
    ws_cr,
    ws_xs,
    ws_xr,
    ws_zs,
    ws_zr,
    ws_full,
    gkv,
    gkv_cr,
    gkv_xs,
    gkv_xr,
    gkv_zs,
    gkv_zr,
    gkv_sum,
    small_0,
    small_cr,
    small_x,
    small_z,
    sems,
):
    net = Links(nz, ny, sems)
    x, y, z, c, other = net.x, net.y, net.z, net.c, net.other
    points = rows_in.shape[0]
    half_z = nz // 2

    barrier = pltpu.get_barrier_semaphore()
    partners = [net.sibling()]
    partners += [net.x_at(d) for d in range(1, NX)]
    partners += [net.y_at(d) for d in range(1, ny)]
    partners += [net.z_at(d) for d in range(1, nz)]
    for device in partners:
        pl.semaphore_signal(barrier, inc=1, device_id=device, device_id_type=MESH)

    spots = lax.broadcasted_iota(jnp.int32, (points, pool_ref.shape[0]), 1)
    chosen = jnp.where(spots == index_ref[...], 1.0, 0.0).astype(BF16)
    rows_buf[y] = dot(chosen, pool_ref[...]).astype(BF16)
    wo_full[y] = w_out_ref[...]
    wh_full[y] = w_hidden_ref[...]
    wl_full[y] = w_logit_ref[...]
    pl.semaphore_wait(barrier, len(partners))

    hub = z % 2 == c
    s_kvx, r_kvx = net.take(1), net.take(1)
    s_kz, r_kz = net.take(nz - 1), net.take(half_z)
    s_kx, r_kx = net.take(NX - 1), net.take(NX - 1)
    s_kc, r_kc = net.take(NX), net.take(NX)
    kv_own = kv_buf.at[c, x, z // 2]

    def kvx_copy():
        return net.copy(kv_ref, kvx, s_kvx, r_kvx, net.sibling())

    def kz_copy(d):
        return net.copy(kv_own, kv_own, s_kz + d - 1, r_kz + z // 2, net.z_at(d))

    @pl.when(jnp.logical_not(hub))
    def _():
        kvx_copy().start()

    s_rows, r_rows = net.take(ny - 1), net.take(ny - 1)
    for d in range(1, ny):
        net.send(rows_buf.at[y], rows_buf.at[y], s_rows + d - 1, r_rows + d - 1, net.y_at(d))

    @pl.when(hub)
    def _():
        net.arrived(kvx, r_kvx)
        own, extra = kv_ref[...], kvx[...]
        low = jnp.where(c == 0, own, extra)
        high = jnp.where(c == 0, extra, own)
        kv_buf[c, x, z // 2] = jnp.concatenate([low, high], axis=0).astype(BF16)
        for d in range(1, nz):
            kz_copy(d).start()

    for d in range(1, ny):
        net.arrived(rows_buf.at[(y + ny - d) % ny], r_rows + d - 1)

    s_wo, r_wo = net.take(ny - 1), net.take(ny - 1)
    s_wh, r_wh = net.take(ny - 1), net.take(ny - 1)
    s_wl, r_wl = net.take(ny - 1), net.take(ny - 1)
    s_fo, r_fo = net.take(ny - 1), net.take(ny - 1)
    s_fh, r_fh = net.take(ny - 1), net.take(ny - 1)
    o_rows, h_rows = w_out_ref.shape[0] // 2, w_hidden_ref.shape[0] // 2

    def wo_half(owner, core):
        return wo_full.at[owner, pl.ds(core * o_rows, o_rows)]

    def wh_half(owner, core):
        return wh_full.at[owner, pl.ds(core * h_rows, h_rows)]

    for d in range(1, ny):
        net.send(wl_full.at[y], wl_full.at[y], s_wl + d - 1, r_wl + d - 1, net.y_at(d))
    for d in range(1, ny):
        net.send(wo_half(y, c), wo_half(y, c), s_wo + d - 1, r_wo + d - 1, net.y_at(d))
    for d in range(1, ny):
        net.send(wh_half(y, c), wh_half(y, c), s_wh + d - 1, r_wh + d - 1, net.y_at(d))

    rows_in[...] = jnp.concatenate([rows_buf[i] for i in range(ny)], axis=1)
    query = dot(rows_in[...], w_query_ref[...]).astype(BF16)
    q_ref[...] = query

    for i in range(half_z):

        @pl.when(jnp.logical_or(z % 2 != c, z // 2 != i))
        def _(i=i):
            net.arrived(kv_buf.at[c, x, i], r_kz + i)

    for d in range(1, NX):
        net.send(kv_buf.at[c, x], kv_buf.at[c, x], s_kx + d - 1, r_kx + d - 1, net.x_at(d))
    for d in range(NX):
        source = (x + NX - d) % NX
        block = kv_buf.at[c, source]
        if d:
            net.arrived(block, r_kx + d - 1)
        net.send(block, block, s_kc + d, r_kc + d, net.sibling())
    for d in range(NX):
        net.arrived(kv_buf.at[other, (x + NX - d) % NX], r_kc + d)

    columns = w_query_ref.shape[1]
    heads = columns // HD
    latents = 16 * half_z * NX * 2
    kv = kv_buf[...].reshape(latents, 2 * columns)
    kv_t = kv.T
    k_all, v_all = kv[:, :columns], kv[:, columns:]
    lane_head = lax.broadcasted_iota(jnp.int32, (points, columns), 1) // HD
    scale = HD ** (-0.5)
    log2e = 1.4426950408889634
    for h in range(heads):
        q_h = jnp.where(lane_head == h, query, jnp.zeros_like(query))
        raw = dot_nt(k_all, q_h)
        top = jnp.max(raw, axis=0, keepdims=True)
        e = jnp.exp2((raw - top) * (scale * log2e))
        p_h = (e * (1.0 / jnp.sum(e, axis=0, keepdims=True))).astype(BF16)
        probs[h] = p_h
        v_t = kv_t[columns + h * HD : columns + (h + 1) * HD]
        att_t[h * HD : (h + 1) * HD] = dot(v_t, p_h).astype(BF16)

    att_buf[y] = att_t[...].T
    s_att, r_att = net.take(ny - 1), net.take(ny - 1)
    for d in range(1, ny):
        net.send(att_buf.at[y], att_buf.at[y], s_att + d - 1, r_att + d - 1, net.y_at(d))

    for d in range(1, ny):
        source = (y + ny - d) % ny
        net.arrived(wo_half(source, c), r_wo + d - 1)
        net.send(wo_half(source, c), wo_half(source, c), s_fo + d - 1, r_fo + d - 1, net.sibling())
    for d in range(1, ny):
        source = (y + ny - d) % ny
        net.arrived(wh_half(source, c), r_wh + d - 1)
        net.send(wh_half(source, c), wh_half(source, c), s_fh + d - 1, r_fh + d - 1, net.sibling())
        net.arrived(wl_full.at[source], r_wl + d - 1)
    for d in range(1, ny):
        source = (y + ny - d) % ny
        net.arrived(wo_half(source, other), r_fo + d - 1)
        net.arrived(att_buf.at[source], r_att + d - 1)

    mixed = rows_in[...].astype(F32)
    for i in range(ny):
        mixed += dot(att_buf[i], wo_full[i])
    center = mixed - jnp.mean(mixed, axis=1, keepdims=True)
    rstd = lax.rsqrt(jnp.mean(center * center, axis=1, keepdims=True) + EPSILON)
    gain = gain_ref[...]
    normal = center * rstd
    normal_ref[...] = normal
    normed_ref[...] = (normal * gain).astype(BF16)

    for d in range(1, ny):
        net.arrived(wh_half((y + ny - d) % ny, other), r_fh + d - 1)

    root = 0.7978845608028654
    cubic = 0.044715
    logit = jnp.zeros((points, 1), F32)
    for i in range(ny):
        v = dot(normed_ref[...], wh_full[i])
        t = jnp.tanh(root * (v + cubic * (v * v * v)))
        act = (0.5 * v * (1.0 + t)).astype(BF16)
        act_ref[i] = act
        slope_ref[i] = 0.5 * (1.0 + t) + 0.5 * v * (1.0 - t * t) * (root * (1.0 + 3.0 * cubic * (v * v)))
        logit += jnp.sum(act.astype(F32) * wl_full[i], axis=1, keepdims=True)
    total_points = points * nz * NX * NC
    d_logit = (jax.nn.sigmoid(logit) - label_ref[...].astype(F32)) * total_points ** (-0.5)
    for i in range(ny):
        dh_ref[i] = (d_logit * wl_full[i] * slope_ref[i]).astype(BF16)
    grad_logit = jnp.sum(d_logit * act_ref[y].astype(F32), axis=0, keepdims=True)

    sums = []
    for i in range(4):
        refs = [r.at[i] for r in (ws_part, ws_cr, ws_xs, ws_xr, ws_zs, ws_zr, ws_full)]
        sums.append(WeightSum(net, refs, i % 2 == 1))
    hidden_1, hidden_2, outs, queries = sums

    normed_t = normed_ref[...].T
    depth = normed_t.shape[0] // 2
    for k, chunk in enumerate((hidden_1, hidden_2)):
        grad = dot(normed_t[k * depth : (k + 1) * depth], dh_ref[y])
        for cc in range(NC):
            for xx in range(NX):
                row = (cc * NX + xx) * 48
                chunk.put(cc, xx, grad[row : row + 48])
        chunk.start()

    d_normed = dot_nt(dh_ref[0], wh_full[0])
    for i in range(1, ny):
        d_normed += dot_nt(dh_ref[i], wh_full[i])
    normal = normal_ref[...]
    both = d_normed * normal
    grad_gain = jnp.sum(both, axis=0, keepdims=True)
    scaled = d_normed * gain
    d_mixed = rstd * (
        scaled
        - jnp.mean(scaled, axis=1, keepdims=True)
        - normal * jnp.mean(both * gain, axis=1, keepdims=True)
    )
    d_mixed = d_mixed.astype(BF16)

    hidden_1.to_x()
    hidden_2.to_x()

    lines = [grad_logit[:, 128 * i : 128 * (i + 1)] for i in range(3)]
    lines += [grad_gain[:, 128 * i : 128 * (i + 1)] for i in range(6)]
    lines += [jnp.zeros((1, 128), F32)]
    for i, line in enumerate(lines):
        small_0[i // 5, i % 5] = line
    s_sc, r_sc = net.take(1), net.take(1)
    s_sx, r_sx = net.take(NX - 1), net.take(NX - 1)
    s_sz, r_sz = net.take(nz - 1), net.take(nz - 1)
    s_sf, r_sf = net.take(1), net.take(1)
    net.send(small_0.at[other], small_cr, s_sc, r_sc, net.sibling())

    def block_rows(chunk, grad):
        for cc in range(NC):
            for xx in range(NX):
                chunk.put(cc, xx, grad[xx * 48 : xx * 48 + 48, cc * 384 : cc * 384 + 384])

    block_rows(outs, dot(att_t[...], d_mixed))
    outs.start()
    w_out = w_out_ref[...]
    d_att = dot_nt(d_mixed, w_out).astype(BF16)
    d_att_t = dot_nt(w_out, d_mixed).astype(BF16)

    net.arrived(small_cr, r_sc)
    small_x[x] = small_0[c] + small_cr[...]
    for d in range(1, NX):
        net.send(small_x.at[x], small_x.at[x], s_sx + d - 1, r_sx + d - 1, net.x_at(d))

    hidden_1.to_z()
    hidden_2.to_z()
    outs.to_x()

    query = q_ref[...]
    kv = kv_buf[...].reshape(latents, 2 * columns)
    kv_t = kv.T
    v_all = kv[:, columns:]
    grad_k = jnp.zeros((latents, columns), F32)
    grad_v = jnp.zeros((latents, columns), F32)
    d_query = []
    for h in range(heads):
        rows = slice(h * HD, (h + 1) * HD)
        p_h = probs[h]
        d_att_h = jnp.where(lane_head == h, d_att, jnp.zeros_like(d_att))
        q_h = jnp.where(lane_head == h, query, jnp.zeros_like(query))
        delta = jnp.sum(d_att_t[rows].astype(F32) * att_t[rows].astype(F32), axis=0, keepdims=True)
        d_probs = dot_nt(v_all, d_att_h)
        d_scores = (p_h.astype(F32) * (d_probs - delta) * scale).astype(BF16)
        d_query.append(dot(kv_t[rows], d_scores).astype(BF16))
        grad_k += dot(d_scores, q_h)
        grad_v += dot(p_h, d_att_h)
    block_rows(queries, dot(jnp.concatenate(d_query, axis=0), rows_in[...]))
    queries.start()
    grads = jnp.concatenate([grad_k, grad_v], axis=1).astype(BF16)
    gkv[...] = grads.reshape(gkv.shape)
    s_gc, r_gc = net.take(1), net.take(1)
    s_gx, r_gx = net.take(NX - 1), net.take(NX - 1)
    s_gz, r_gz = net.take(half_z), net.take(nz - 1)
    s_gf, r_gf = net.take(1), net.take(1)
    net.send(gkv.at[other], gkv_cr, s_gc, r_gc, net.sibling())

    queries.to_x()
    hidden_1.back_z()
    hidden_2.back_z()
    outs.to_z()

    for d in range(1, NX):
        net.arrived(small_x.at[(x + NX - d) % NX], r_sx + d - 1)
    line = small_x[0]
    for i in range(1, NX):
        line += small_x[i]
    small_z[z] = line
    for d in range(1, nz):
        net.send(small_z.at[z], small_z.at[z], s_sz + d - 1, r_sz + d - 1, net.z_at(d))

    net.arrived(gkv_cr, r_gc)
    gkv_xs[...] = (gkv[c].astype(F32) + gkv_cr[...].astype(F32)).astype(BF16)
    for d in range(1, NX):
        net.send(
            gkv_xs.at[(x + d) % NX], gkv_xr.at[d - 1], s_gx + d - 1, r_gx + d - 1, net.x_at(d)
        )

    queries.to_z()
    hidden_1.back_x()
    hidden_2.back_x()
    outs.back_z()

    total = gkv_xs[x].astype(F32)
    for d in range(1, NX):
        net.arrived(gkv_xr.at[d - 1], r_gx + d - 1)
        total += gkv_xr[d - 1].astype(F32)
    gkv_zs[...] = total.astype(BF16)
    for i in range(half_z):
        target = 2 * i + c
        way = (target - z + nz) % nz

        def copy(i=i, target=target, way=way):
            return net.copy(
                gkv_zs.at[i], gkv_zr.at[way - 1], s_gz + i, r_gz + way - 1, net.at(z=target)
            )

        @pl.when(way != 0)
        def _(copy=copy):
            copy().start()

        @net.ends.append
        def _(copy=copy, way=way):
            @pl.when(way != 0)
            def _():
                copy().wait_send()

    queries.back_z()
    hidden_1.back_core()
    hidden_2.back_core()
    outs.back_x()

    for d in range(1, nz):
        net.arrived(small_z.at[(z + nz - d) % nz], r_sz + d - 1)
    line = small_z[0]
    for i in range(1, nz):
        line += small_z[i]
    small_ref[c] = line
    net.send(small_ref.at[c], small_ref.at[c], s_sf, r_sf, net.sibling())

    queries.back_x()

    def gf_copy():
        return net.copy(
            gkv_sum.at[other], okv_ref, s_gf, r_gf, net.sibling()
        )

    @pl.when(hub)
    def _():
        total = gkv_zs[z // 2].astype(F32)
        for d in range(1, nz):
            net.arrived(gkv_zr.at[d - 1], r_gz + d - 1)
            total += gkv_zr[d - 1].astype(F32)
        gkv_sum[...] = total.reshape(gkv_sum.shape)
        gf_copy().start()
        okv_ref[...] = gkv_sum[c]

    outs.back_core()
    queries.back_core()

    for chunk, first in ((hidden_1, 0), (hidden_2, depth)):
        chunk.end()
        for cc in range(NC):
            for xx in range(NX):
                row = first + (cc * NX + xx) * 48
                owh_ref[row : row + 48, :] = chunk.block(cc, xx)
    for chunk, ref in ((outs, owo_ref), (queries, owq_ref)):
        chunk.end()
        for cc in range(NC):
            for xx in range(NX):
                ref[xx * 48 : xx * 48 + 48, cc * 384 : cc * 384 + 384] = chunk.block(cc, xx)

    @pl.when(jnp.logical_not(hub))
    def _():
        net.arrived(okv_ref, r_gf)

    net.arrived(small_ref.at[other], r_sf)

    @pl.when(hub)
    def _():
        for d in range(1, nz):
            kz_copy(d).wait_send()
        gf_copy().wait_send()

    @pl.when(jnp.logical_not(hub))
    def _():
        kvx_copy().wait_send()

    net.finish()


def solution(mesh):
    nz = mesh.shape["pts"] // (NX * NC)
    ny = mesh.shape["head"]
    half_z = nz // 2

    def on_device(pool, index, labels, w_query, keys, values, w_out, out_gain, w_hidden, w_logit):
        points, columns = index.shape[0], keys.shape[1]
        width, hidden = w_hidden.shape
        latents = keys.shape[0] * nz * NX * NC
        heads = columns // HD
        kv = jnp.concatenate([keys, values], axis=1).astype(F32)
        vmem = pltpu.VMEM
        tile = (16, 128)
        wide = (16, 2 * columns)
        scratch = [
            vmem((ny, points, columns), BF16),
            vmem((points, width), BF16),
            vmem((ny, columns, width), BF16),
            vmem((ny, width, hidden), BF16),
            vmem((ny, 1, hidden), F32),
            vmem((8, 2 * columns), F32),
            vmem((2, NX, half_z) + wide, BF16),
            vmem((points, columns), BF16),
            vmem((heads, latents, points), BF16),
            vmem((columns, points), BF16),
            vmem((ny, points, columns), BF16),
            vmem((points, width), F32),
            vmem((points, width), BF16),
            vmem((ny, points, hidden), BF16),
            vmem((ny, points, hidden), F32),
            vmem((ny, points, hidden), BF16),
            vmem((4, NC, NX, PIECES) + tile, BF16),
            vmem((4, NX, PIECES) + tile, BF16),
            vmem((4, NX, PIECES) + tile, BF16),
            vmem((4, NX - 1, PIECES) + tile, BF16),
            vmem((4, PIECES) + tile, BF16),
            vmem((4, nz - 1) + tile, BF16),
            vmem((4, NC, NX, PIECES) + tile, BF16),
            vmem((2, NX, half_z) + wide, BF16),
            vmem((NX, half_z) + wide, BF16),
            vmem((NX, half_z) + wide, BF16),
            vmem((NX - 1, half_z) + wide, BF16),
            vmem((half_z,) + wide, BF16),
            vmem((nz - 1,) + wide, BF16),
            vmem((2, 8, 2 * columns), F32),
            vmem((NC, 5, 1, 128), F32),
            vmem((5, 1, 128), F32),
            vmem((NX, 5, 1, 128), F32),
            vmem((nz, 5, 1, 128), F32),
            pltpu.SemaphoreType.DMA((512,)),
        ]
        shapes = [
            jax.ShapeDtypeStruct((width, hidden), BF16),
            jax.ShapeDtypeStruct((columns, width), BF16),
            jax.ShapeDtypeStruct((columns, width), BF16),
            jax.ShapeDtypeStruct((NC, 5, 1, 128), F32),
            jax.ShapeDtypeStruct((8, 2 * columns), F32),
        ]
        whole = pl.BlockSpec(memory_space=pltpu.VMEM)
        grad_wh, grad_wo, grad_wq, small, grad_kv = pl.pallas_call(
            lambda *refs: kernel(nz, ny, *refs),
            out_shape=shapes,
            in_specs=[whole] * 9,
            out_specs=[whole] * 5,
            scratch_shapes=scratch,
            compiler_params=pltpu.CompilerParams(
                collective_id=0, has_side_effects=True, vmem_limit_bytes=60 * 1024 * 1024
            ),
        )(
            pool,
            index.reshape(points, 1),
            labels.reshape(points, 1),
            w_query,
            kv,
            w_out,
            out_gain.astype(F32).reshape(1, width),
            w_hidden,
            w_logit.astype(F32).reshape(1, hidden),
        )
        small = small.reshape(-1)
        return (
            grad_wq.T.astype(F32),
            grad_wo.astype(F32),
            grad_wh.astype(F32),
            small[:hidden],
            small[hidden : hidden + width],
            grad_kv[:, :columns],
            grad_kv[:, columns:],
        )

    return jax.shard_map(
        on_device,
        mesh=mesh,
        in_specs=(
            P("pts", "head"),
            P("pts"),
            P("pts"),
            P(None, "head"),
            P("pts", "head"),
            P("pts", "head"),
            P("head", None),
            P(),
            P(None, "head"),
            P("head"),
        ),
        out_specs=(
            P(None, "head"),
            P("head", None),
            P(None, "head"),
            P("head"),
            P(),
            P("pts", "head"),
            P("pts", "head"),
        ),
        check_vma=False,
    )
```

time: 723 us -> 119 us (0.16)
  blocking collectives: 449 us -> 0 us
  waiting for transfers between devices: 215 us -> 0 us
  Pallas kernels: 0 us -> 104 us
  matrix products: 18.3 us -> 0 us
  between operations: 14.7 us -> 0.72 us
    psum x2 -> x0, blocking collectives: 263 us -> none  [the longest x1 255 us: on_device(): lax.psum((grad_wq, grad_wo, grad_w1, grad_w2, grad_g), 'pts')]
    psum x3 -> x0, waiting for transfers between devices: 214 us -> none  [the longest x1 103 us: on_device(): lax.psum((grad_wq, grad_wo, grad_w1, grad_w2, grad_g), 'pts')]
    all_gather x3 -> x0, blocking collectives: 186 us -> none  [the longest x1 93 us: on_device(): lax.all_gather(keys, 'pts', axis=0, tiled=True)]
    pallas_call x0 -> x1, Pallas kernels: none -> 104 us  [on_device(): pl.pallas_call(lambda *refs: kernel(nz, ny, *refs), out_shape=shapes, in_...]
    dot_general x15 -> x0, matrix products: 15.3 us -> none  [the longest x1 2.91 us: on_device(): jnp.einsum('pd,pf->df', normed, d_hidden, preferred_element_type=jnp.floa...]
  transfers between devices with their start and end apart: 3 -> 0, of which waited for: 3 -> 0; matrix products, arithmetic and copies ran while one was open for 1% -> 0% of each run, Pallas kernels for 0% -> 0%
where the time goes in v1:
time: 119 us
  Pallas kernels  104 us (87%)
  local copies, waits for them, and re-layouts  9.06 us (8%)
  other arithmetic  5.33 us (4%)
    pallas_call x1, Pallas kernels, on_device(): pl.pallas_call(lambda *refs: kernel(nz, ny, *refs), out_shape=shapes, in_...  104 us
    unnamed x18, local copies, waits for them, and re-layouts  3.76 us

profile of v1, /device:TPU:1, one launch (start us, length us, event | category | flops | bytes accessed | tf_op | source)
XLA Modules:
  0.0 119.1 jit_solution(10109607969364079032)
XLA Ops:
  0.6 0.0 copy-start.4
  0.6 0.0 copy-start.5
  0.7 0.0 copy-start.3
  0.7 0.0 copy-start.2
  0.7 0.0 copy-start.6
  0.7 0.0 copy-start.7
  0.7 1.9 %copy.22.refs_3_ = bf16[768,192]{1,0:T(8,128)(2,1)} copy(bf16[768,192]{0,1:T(8,128)(2,1)} %param.13) | data formatting | bytes 589824 | tf_op args[3]
  2.6 1.8 %copy.19.refs_0_ = bf16[576,192]{1,0:T(8,128)(2,1)} copy(bf16[576,192]{0,1:T(8,128)(2,1)} %param.10) | data formatting | bytes 442368 | tf_op args[0]
  4.4 0.8 reshape.44.refs_1_
  5.2 0.0 copy-done.5
  5.2 0.8 reshape.45.refs_2_
  6.0 0.0 copy-done.2
  6.0 0.7 maximum_convert_fusion.refs_4_
  6.6 0.0 copy-done.6
  6.6 0.6 reshape.41.refs_6_
  7.2 0.6 reshape.43.refs_8_
  7.8 104.0 %shard_map.153 = (bf16[768,384]{1,0:T(8,128)(2,1)}, bf16[192,768]{1,0:T(8,128)(2,1)}, bf16[192,768]{1,0:T(8,128)(2,1)}, f32[2,5,1,128]{3,2,1,0:T(1,128)}, f32[8,384]{1,0:T(8,128)}) custom-call(bf16[576,192]{1,0:T(8,128)(2,1)} %copy.19.refs_0_, s32[288,1]{1,0:T(8,128)} %reshape.44.refs_1_, s32[288,1]{1,0:T(8,128)} %reshape.45.refs_2_, ...), custom_call_target="tpu_custom_call" | custom-call | tf_op jit(solution)/shard_map/pallas_call | solution.py:688
  111.8 0.8 reduce
  112.6 0.6 slice.17
  113.2 0.6 slice.16
  113.8 1.4 %fusion = (f32[8,192]{1,0:T(8,128)}, f32[8,192]{1,0:T(8,128)}) fusion(f32[8,384]{1,0:T(8,128)} %get-tuple-element.16), kind=kLoop, calls=%fused_computation.2 | loop fusion | bytes 24576 | tf_op jit(solution)/shard_map/slice | solution.py:716
  115.2 2.2 %convert_element_type.21 = f32[768,384]{1,0:T(8,128)} convert(bf16[768,384]{1,0:T(8,128)(2,1)} %get-tuple-element.14) | non-fusion elementwise | flops 294912 | bytes 1769472 | tf_op jit(solution)/shard_map/convert_element_type | solution.py:712
  117.4 0.9 convert_bitcast_fusion
  118.3 0.9 convert_element_type.20
  (8 shorter events, 0.0 us)
Async XLA Ops:
  0.6 3.8 %copy-start.4 = (s32[288]{0:T(512)S(1)}, s32[288]{0:T(512)}, u32[]{:S(2)}) copy-start(s32[288]{0:T(512)} %param.11) | copy-start | bytes 3460
  0.6 4.5 %copy-start.5 = (s32[288]{0:T(512)S(1)}, s32[288]{0:T(512)}, u32[]{:S(2)}) copy-start(s32[288]{0:T(512)} %param.12) | copy-start | bytes 3460
  0.7 5.3 %copy-start.3 = (bf16[8,192]{1,0:T(8,128)(2,1)S(1)}, bf16[8,192]{1,0:T(8,128)(2,1)}, u32[]{:S(2)}) copy-start(bf16[8,192]{1,0:T(8,128)(2,1)} %param.14) | copy-start | bytes 9220
  0.7 5.3 %copy-start.2 = (bf16[8,192]{1,0:T(8,128)(2,1)S(1)}, bf16[8,192]{1,0:T(8,128)(2,1)}, u32[]{:S(2)}) copy-start(bf16[8,192]{1,0:T(8,128)(2,1)} %param.15) | copy-start | bytes 9220
  0.7 6.0 %copy-start.6 = (bf16[768]{0:T(1024)(128)(2,1)S(1)}, bf16[768]{0:T(1024)(128)(2,1)}, u32[]{:S(2)}) copy-start(bf16[768]{0:T(1024)(128)(2,1)} %param.17) | copy-start | bytes 4612
  0.7 6.5 %copy-start.7 = (bf16[384]{0:T(512)(128)(2,1)S(1)}, bf16[384]{0:T(512)(128)(2,1)}, u32[]{:S(2)}) copy-start(bf16[384]{0:T(512)(128)(2,1)} %param.19) | copy-start | bytes 2308
  111.8 5.6 %copy-start.1 = (bf16[192,768]{1,0:T(8,128)(2,1)S(1)}, bf16[192,768]{1,0:T(8,128)(2,1)}, u32[]{:S(2)}) copy-start(bf16[192,768]{1,0:T(8,128)(2,1)} %get-tuple-element.12) | copy-start | bytes 884740
  115.2 3.1 %copy-start = (bf16[192,768]{1,0:T(8,128)(2,1)S(1)}, bf16[192,768]{1,0:T(8,128)(2,1)}, u32[]{:S(2)}) copy-start(bf16[192,768]{1,0:T(8,128)(2,1)} %get-tuple-element.13) | copy-start | bytes 884740

commit v2 on v1

v2 whole, which is shorter than its diff:
```python
import jax
import jax.numpy as jnp
from jax import lax
from jax.experimental import pallas as pl
from jax.experimental.pallas import tpu as pltpu
from jax.sharding import PartitionSpec as P

HD = 64
EPSILON = 1e-05
NX = 4
NC = 2
PIECES = 9
SEMAPHORES = 112
MESH = pl.DeviceIdType.MESH
F32 = jnp.float32
BF16 = jnp.bfloat16


def dot(a, b):
    return jnp.dot(a, b, preferred_element_type=F32)


def dot_nt(a, b):
    return lax.dot_general(a, b, (((1,), (1,)), ((), ())), preferred_element_type=F32)


def far_first(n):
    return sorted(range(1, n), key=lambda d: -min(d, n - d))


def packed(block):
    half = block.shape[0] // 2
    return block[:, :128], jnp.concatenate([block[:half, 128:], block[half:, 128:]], axis=1)


def folded(block):
    half = block.shape[0] // 2
    return jnp.concatenate([block[:half], block[half:]], axis=1)


def unfolded(block):
    return jnp.concatenate([block[:, :64], block[:, 64:]], axis=0)


def unpacked(wide, narrow):
    return jnp.concatenate([wide, jnp.concatenate([narrow[:, :64], narrow[:, 64:]], axis=0)], axis=1)


class Links:
    def __init__(self, nz, ny, sems):
        self.nz, self.ny, self.sems, self.used = nz, ny, sems, 0
        p = lax.axis_index("pts")
        self.y = lax.axis_index("head")
        self.c = p % NC
        self.x = (p // NC) % NX
        self.z = p // (NC * NX)
        self.other = 1 - self.c
        self.ends = []

    def at(self, x=None, y=None, z=None, c=None):
        x = self.x if x is None else x
        y = self.y if y is None else y
        z = self.z if z is None else z
        c = self.c if c is None else c
        return (z * (NC * NX) + x * NC + c, y)

    def x_at(self, d):
        return self.at(x=(self.x + d) % NX)

    def y_at(self, d):
        return self.at(y=(self.y + d) % self.ny)

    def z_at(self, d):
        return self.at(z=(self.z + d) % self.nz)

    def sibling(self):
        return self.at(c=self.other)

    def take(self, count):
        first = self.used
        self.used += count
        return first

    def copy(self, src, dst, send, recv, device):
        return pltpu.make_async_remote_copy(
            src_ref=src,
            dst_ref=dst,
            send_sem=self.sems.at[send],
            recv_sem=self.sems.at[recv if isinstance(recv, int) else sum(recv)],
            device_id=device,
            device_id_type=MESH,
        )

    def pair(self):
        return self.take(1), self.take(1)

    def send(self, src, dst, pair, device):
        self.copy(src, dst, pair[0], pair[1], device).start()

    def arrived(self, total, recv):
        self.copy(total, total, 0, recv, self.sibling()).wait_recv()

    def sent(self, total, pair):
        self.copy(total, total, pair[0], 0, self.sibling()).wait_send()

    def later(self, total, pair):
        self.ends.append(lambda: self.sent(total, pair))

    def finish(self):
        for end in self.ends:
            end()


class WeightSum:
    def __init__(self, net, refs, mirrored):
        self.net, self.mirrored = net, mirrored
        self.part, self.cr, self.xs, self.xr, self.zs, self.zr, self.full = refs
        nz = net.nz
        self.core, self.x, self.z = net.pair(), net.pair(), net.pair()
        self.gz, self.gx, self.gc = net.pair(), net.pair(), net.pair()
        self.piece, self.reduces = self.role(net.z)

    def role(self, z):
        nz = self.net.nz
        spot = (nz - 1 - z) if self.mirrored else z
        piece = (PIECES * spot + nz - 1) // nz
        return jnp.minimum(piece, PIECES - 1), (nz * piece) // PIECES == spot

    def owner(self, piece):
        spot = (self.net.nz * piece) // PIECES
        return self.net.nz - 1 - spot if self.mirrored else spot

    def put(self, c, x, block):
        block = block.astype(BF16)
        for j in range(PIECES):
            r, l = 16 * (j // 3), 128 * (j % 3)
            self.part[c, x, j] = block[r : r + 16, l : l + 128]

    def start(self):
        net = self.net
        net.send(self.part.at[net.other], self.cr, self.core, net.sibling())
        net.later(self.cr, self.core)

    def to_x(self):
        net = self.net
        net.arrived(self.cr, self.core[1])
        self.xs[...] = (self.part[net.c].astype(F32) + self.cr[...].astype(F32)).astype(BF16)
        for d in far_first(NX):
            target = (net.x + d) % NX
            net.send(self.xs.at[target], self.xr.at[d - 1], self.x, net.x_at(d))
        net.later(self.xr, self.x)

    def to_z(self):
        net = self.net
        net.arrived(self.xr, self.x[1])
        total = self.xs[net.x].astype(F32)
        for d in range(1, NX):
            total += self.xr[d - 1].astype(F32)
        self.zs[...] = total.astype(BF16)
        for d in far_first(net.nz):
            spot = (net.z + d) % net.nz
            piece, reduces = self.role(spot)

            @pl.when(reduces)
            def _(d=d, piece=piece, spot=spot):
                net.send(self.zs.at[piece], self.zr.at[d - 1], self.z, net.at(z=spot))

        @net.ends.append
        def _():
            self.pieces(lambda total: net.sent(total, self.z))

    def pieces(self, wait):
        @pl.when(self.reduces)
        def _():
            wait(self.zs.at[pl.ds(0, PIECES - 1)])

        @pl.when(jnp.logical_not(self.reduces))
        def _():
            wait(self.zs)

    def back_z(self):
        net = self.net
        tile = self.full.at[net.c, net.x, self.piece]

        @pl.when(self.reduces)
        def _():
            net.arrived(self.zr, self.z[1])
            total = self.zs[self.piece].astype(F32)
            for d in range(1, net.nz):
                total += self.zr[d - 1].astype(F32)
            self.full[net.c, net.x, self.piece] = total.astype(BF16)
            for d in far_first(net.nz):
                net.send(tile, tile, self.gz, net.z_at(d))

        @net.ends.append
        def _():
            @pl.when(self.reduces)
            def _():
                net.sent(self.zr, self.gz)

    def back_x(self):
        net = self.net
        self.pieces(lambda total: net.arrived(total, self.gz[1]))
        mine = self.full.at[net.c, net.x]
        for d in far_first(NX):
            net.send(mine, mine, self.gx, net.x_at(d))
        net.later(self.xr, self.gx)

    def back_core(self):
        net = self.net
        net.arrived(self.xr, self.gx[1])
        mine = self.full.at[net.c]
        net.send(mine, mine, self.gc, net.sibling())
        net.later(mine, self.gc)

    def end(self):
        net = self.net
        net.arrived(self.full.at[net.other], self.gc[1])


def kernel(
    nz,
    ny,
    pool_hbm,
    index_hbm,
    label_hbm,
    gain_hbm,
    w_logit_hbm,
    w_query_hbm,
    keys_hbm,
    values_hbm,
    w_out_hbm,
    w_hidden_hbm,
    ws_hbm,
    small_hbm,
    okv_hbm,
    ws_full,
    small_ref,
    okv_ref,
    pool,
    index,
    label_ref,
    gain_ref,
    w_logit,
    w_query,
    keys,
    values,
    rows_wide,
    rows_narrow,
    rows_in,
    wo_full,
    wh_full,
    wl_full,
    kv_own,
    kvx,
    kv_buf,
    q_ref,
    probs,
    att_t,
    att_buf,
    kv_t_ref,
    ds_ref,
    normal_ref,
    normed_ref,
    act_ref,
    slope_ref,
    dh_ref,
    ws_part,
    ws_cr,
    ws_xs,
    ws_xr,
    ws_zs,
    ws_zr,
    gkv,
    gkv_cr,
    gkv_xs,
    gkv_xr,
    gkv_zs,
    gkv_zr,
    gkv_sum,
    small_0,
    small_cr,
    small_x,
    small_z,
    local,
    sems,
):
    net = Links(nz, ny, sems)
    x, y, z, c, other = net.x, net.y, net.z, net.c, net.other
    points, width = rows_in.shape
    half_z = nz // 2
    hidden = wh_full.shape[2]

    barrier = pltpu.get_barrier_semaphore()
    partners = [net.sibling()]
    partners += [net.x_at(d) for d in range(1, NX)]
    partners += [net.y_at(d) for d in range(1, ny)]
    partners += [net.z_at(d) for d in far_first(nz)]
    for device in partners:
        pl.semaphore_signal(barrier, inc=1, device_id=device, device_id_type=MESH)

    loads = [
        pltpu.make_async_copy(source, target, local.at[i])
        for i, (source, target) in enumerate(
            (
                (keys_hbm, keys),
                (values_hbm, values),
                (index_hbm, index),
                (pool_hbm, pool),
                (w_out_hbm, wo_full.at[y]),
                (w_hidden_hbm, wh_full.at[y]),
                (w_query_hbm, w_query),
                (label_hbm, label_ref),
                (gain_hbm, gain_ref),
                (w_logit_hbm, w_logit),
            )
        )
    ]
    for load in loads:
        load.start()
    loads[0].wait()
    loads[1].wait()
    kv_own[...] = jnp.concatenate([keys[...].astype(F32), values[...].astype(F32)], axis=1)
    pl.semaphore_wait(barrier, len(partners))

    hub = z % 2 == c
    kvx_pair, kx_pair, kc_pair = net.pair(), net.pair(), net.pair()
    s_kz, r_kz = net.take(1), net.take(half_z)
    kv_tile = kv_buf.at[c, x, z // 2]

    @pl.when(jnp.logical_not(hub))
    def _():
        net.send(kv_own, kvx, kvx_pair, net.sibling())

    loads[2].wait()
    loads[3].wait()
    spots = lax.broadcasted_iota(jnp.int32, (pool.shape[1], points), 0)
    chosen = jnp.where(spots == index[...].reshape(1, points), 1.0, 0.0).astype(BF16)
    picked = dot(pool[...], chosen).T.astype(BF16)
    wide, narrow = packed(picked)
    rows_wide[y] = wide
    rows_narrow[y] = narrow

    wide_pair, narrow_pair = net.pair(), net.pair()
    for d in far_first(ny):
        net.send(rows_wide.at[y], rows_wide.at[y], wide_pair, net.y_at(d))
        net.send(rows_narrow.at[y], rows_narrow.at[y], narrow_pair, net.y_at(d))
    others = pl.ds(0, ny - 1)
    net.later(rows_wide.at[others], wide_pair)
    net.later(rows_narrow.at[others], narrow_pair)

    @pl.when(hub)
    def _():
        net.arrived(kvx, kvx_pair[1])
        own, extra = kv_own[...], kvx[...]
        low = jnp.where(c == 0, own, extra)
        high = jnp.where(c == 0, extra, own)
        kv_buf[c, x, z // 2] = jnp.concatenate([low, high], axis=0).astype(BF16)
        for d in far_first(nz):
            net.send(kv_tile, kv_tile, (s_kz, (r_kz, z // 2)), net.z_at(d))

    @net.ends.append
    def _():
        @pl.when(hub)
        def _():
            net.sent(gkv_zr, (s_kz, 0))

        @pl.when(jnp.logical_not(hub))
        def _():
            net.sent(kv_own, kvx_pair)

    wo_pair, near_pair, far_pair, wl_pair = net.pair(), net.pair(), net.pair(), net.pair()
    wx_pair, fo_pair, fn_pair, ff_pair = net.pair(), net.pair(), net.pair(), net.pair()
    o_rows, h_rows = wo_full.shape[1] // 2, wh_full.shape[1] // 2
    x_rows = h_rows // NX
    far = ny // 2

    def wo_half(owner, core):
        return wo_full.at[owner, pl.ds(core * o_rows, o_rows)]

    def wh_half(owner, core):
        return wh_full.at[owner, pl.ds(core * h_rows, h_rows)]

    def wh_part(owner, core, part):
        return wh_full.at[owner, pl.ds(core * h_rows + part * x_rows, x_rows)]

    def wo_bytes(count):
        return wo_full.at[pl.ds(0, count), pl.ds(0, o_rows)]

    def wh_bytes(count):
        return wh_full.at[pl.ds(0, count), pl.ds(0, h_rows)]

    loads[4].wait()
    for d in far_first(ny):
        net.send(wo_half(y, c), wo_half(y, c), wo_pair, net.y_at(d))
    net.later(wo_bytes(ny - 1), wo_pair)
    loads[5].wait()
    loads[9].wait()
    wl_full[y] = w_logit[...].astype(F32).reshape(1, hidden)
    for d in far_first(ny):
        if d == far:
            net.send(wh_part(y, c, x), wh_part(y, c, x), far_pair, net.y_at(d))
        else:
            net.send(wh_half(y, c), wh_half(y, c), near_pair, net.y_at(d))
        net.send(wl_full.at[y], wl_full.at[y], wl_pair, net.y_at(d))
    net.later(wh_part(0, 0, 0), far_pair)
    net.later(wh_bytes(ny - 2), near_pair)
    net.later(wl_full.at[others], wl_pair)

    side = jnp.where(jnp.logical_and(z % 2 == 0, c == 1), half_z - 1, 1)
    blocks = []
    for k in range(half_z):
        away = (k + 1) // 2
        step = away * side if k % 2 else (half_z - away) * side
        block = (z // 2 + step) % half_z
        blocks.append(block)
        tile = kv_buf.at[c, x, block]
        if k:
            net.arrived(tile, (r_kz, block))
        else:

            @pl.when(jnp.logical_not(hub))
            def _(tile=tile, block=block):
                net.arrived(tile, (r_kz, block))

        for d in far_first(NX):
            net.send(tile, tile, kx_pair, net.x_at(d))
    net.later(gkv_xr, kx_pair)
    net.arrived(rows_wide.at[others], wide_pair[1])
    net.arrived(rows_narrow.at[others], narrow_pair[1])
    rows_in[...] = jnp.concatenate(
        [unpacked(rows_wide[i], rows_narrow[i]) for i in range(ny)], axis=1
    )
    loads[6].wait()
    query = dot_nt(rows_in[...], w_query[...]).astype(BF16)
    q_ref[...] = query
    own = kv_buf.at[c, x]
    net.send(own, own, kc_pair, net.sibling())
    net.arrived(gkv_xr, kx_pair[1])
    for d in range(1, NX):
        block = kv_buf.at[c, (x + NX - d) % NX]
        net.send(block, block, kc_pair, net.sibling())
    net.later(gkv_xs, kc_pair)
    net.arrived(gkv_xs, kc_pair[1])

    columns = w_query.shape[0]
    heads = columns // HD
    latents = 16 * half_z * NX * 2
    kv = kv_buf[...].reshape(latents, 2 * columns)
    kv_t_ref[...] = kv.T
    k_all, v_all = kv[:, :columns], kv[:, columns:]
    att_pair = net.pair()
    lane_head = lax.broadcasted_iota(jnp.int32, (points, columns), 1) // HD
    scale = HD ** (-0.5)
    log2e = 1.4426950408889634
    for h in range(heads):
        q_h = jnp.where(lane_head == h, query, jnp.zeros_like(query))
        raw = dot_nt(k_all, q_h)
        top = jnp.max(raw, axis=0, keepdims=True)
        e = jnp.exp2((raw - top) * (scale * log2e))
        p_h = (e * (1.0 / jnp.sum(e, axis=0, keepdims=True))).astype(BF16)
        probs[h] = p_h
        v_t = kv_t_ref[columns + h * HD : columns + (h + 1) * HD]
        att_h = dot(v_t, p_h).astype(BF16)
        att_t[h * HD : (h + 1) * HD] = att_h
        att_buf[y, h] = folded(att_h.T)
        for d in far_first(ny):
            net.send(att_buf.at[y, h], att_buf.at[y, h], att_pair, net.y_at(d))

    net.later(att_buf.at[others], att_pair)
    far_y = (y + ny - far) % ny
    net.arrived(wo_bytes(ny - 1), wo_pair[1])
    for d in range(1, ny):
        block = wo_half((y + ny - d) % ny, c)
        net.send(block, block, fo_pair, net.sibling())
    net.later(wo_bytes(ny - 1), fo_pair)
    net.arrived(wh_part(0, 0, 0), far_pair[1])
    for d in far_first(NX):
        net.send(wh_part(far_y, c, x), wh_part(far_y, c, x), wx_pair, net.x_at(d))
    three = wh_full.at[0, pl.ds(0, (NX - 1) * x_rows)]
    net.later(three, wx_pair)
    net.arrived(wl_full.at[others], wl_pair[1])
    net.arrived(wh_bytes(ny - 2), near_pair[1])
    for d in range(1, ny):
        if d != far:
            block = wh_half((y + ny - d) % ny, c)
            net.send(block, block, fn_pair, net.sibling())
    net.later(wh_bytes(ny - 2), fn_pair)
    net.arrived(three, wx_pair[1])
    net.send(wh_half(far_y, c), wh_half(far_y, c), ff_pair, net.sibling())
    net.later(wh_half(0, 0), ff_pair)
    net.arrived(wo_bytes(ny - 1), fo_pair[1])
    net.arrived(att_buf.at[others], att_pair[1])

    attended = jnp.concatenate(
        [unfolded(att_buf[i, h]) for i in range(ny) for h in range(heads)], axis=1
    )
    mixed = rows_in[...].astype(F32) + dot(attended, wo_full[...].reshape(width, width))
    center = mixed - jnp.mean(mixed, axis=1, keepdims=True)
    rstd = lax.rsqrt(jnp.mean(center * center, axis=1, keepdims=True) + EPSILON)
    loads[8].wait()
    gain = gain_ref[...].astype(F32).reshape(1, width)
    normal = center * rstd
    normal_ref[...] = normal
    normed_ref[...] = (normal * gain).astype(BF16)

    net.arrived(wh_bytes(ny - 2), fn_pair[1])
    net.arrived(wh_half(0, 0), ff_pair[1])

    root = 0.7978845608028654
    cubic = 0.044715
    logit = jnp.zeros((points, 1), F32)
    for i in range(ny):
        v = dot(normed_ref[...], wh_full[i])
        t = jnp.tanh(root * (v + cubic * (v * v * v)))
        act = (0.5 * v * (1.0 + t)).astype(BF16)
        act_ref[i] = act
        slope_ref[i] = 0.5 * (1.0 + t) + 0.5 * v * (1.0 - t * t) * (root * (1.0 + 3.0 * cubic * (v * v)))
        logit += jnp.sum(act.astype(F32) * wl_full[i], axis=1, keepdims=True)
    total_points = points * nz * NX * NC
    loads[7].wait()
    label = label_ref[...].astype(F32).reshape(1, points)
    label = jnp.broadcast_to(label, (8, points)).T[:, 0:1]
    d_logit = (jax.nn.sigmoid(logit) - label) * total_points ** (-0.5)
    for i in range(ny):
        dh_ref[i] = (d_logit * wl_full[i] * slope_ref[i]).astype(BF16)

    sums = []
    for i in range(4):
        refs = [r.at[i] for r in (ws_part, ws_cr, ws_xs, ws_xr, ws_zs, ws_zr, ws_full)]
        sums.append(WeightSum(net, refs, i % 2 == 1))
    hidden_1, hidden_2, outs, queries = sums

    normed_t = normed_ref[...].T
    depth = normed_t.shape[0] // 2
    for k, chunk in enumerate((hidden_1, hidden_2)):
        grad = dot(normed_t[k * depth : (k + 1) * depth], dh_ref[y])
        for cc in range(NC):
            for xx in range(NX):
                row = (cc * NX + xx) * 48
                chunk.put(cc, xx, grad[row : row + 48])
        chunk.start()
    grad_logit = jnp.sum(d_logit * act_ref[y].astype(F32), axis=0, keepdims=True)

    d_normed = dot_nt(dh_ref[0], wh_full[0])
    for i in range(1, ny):
        d_normed += dot_nt(dh_ref[i], wh_full[i])
    normal = normal_ref[...]
    both = d_normed * normal
    grad_gain = jnp.sum(both, axis=0, keepdims=True)
    scaled = d_normed * gain
    d_mixed = rstd * (
        scaled
        - jnp.mean(scaled, axis=1, keepdims=True)
        - normal * jnp.mean(both * gain, axis=1, keepdims=True)
    )
    d_mixed = d_mixed.astype(BF16)

    hidden_1.to_x()
    hidden_2.to_x()

    lines = [grad_logit[:, 128 * i : 128 * (i + 1)] for i in range(3)]
    lines += [grad_gain[:, 128 * i : 128 * (i + 1)] for i in range(6)]
    lines += [jnp.zeros((1, 128), F32)]
    for i, line in enumerate(lines):
        small_0[i // 5, i % 5] = line
    sc_pair, sx_pair, sz_pair, sf_pair = net.pair(), net.pair(), net.pair(), net.pair()
    net.send(small_0.at[other], small_cr, sc_pair, net.sibling())
    net.later(small_cr, sc_pair)

    def block_rows(chunk, grad):
        for cc in range(NC):
            for xx in range(NX):
                chunk.put(cc, xx, grad[xx * 48 : xx * 48 + 48, cc * 384 : cc * 384 + 384])

    w_out = wo_full[y]
    d_att = dot_nt(d_mixed, w_out).astype(BF16)
    d_att_t = dot_nt(w_out, d_mixed).astype(BF16)

    query = q_ref[...]
    v_all = kv_buf[...].reshape(latents, 2 * columns)[:, columns:]
    d_query = []
    for h in range(heads):
        rows = slice(h * HD, (h + 1) * HD)
        d_att_h = jnp.where(lane_head == h, d_att, jnp.zeros_like(d_att))
        delta = jnp.sum(d_att_t[rows].astype(F32) * att_t[rows].astype(F32), axis=0, keepdims=True)
        d_probs = dot_nt(v_all, d_att_h)
        d_scores = (probs[h].astype(F32) * (d_probs - delta) * scale).astype(BF16)
        ds_ref[h] = d_scores
        d_query.append(dot(kv_t_ref[rows], d_scores).astype(BF16))
    block_rows(queries, dot(jnp.concatenate(d_query, axis=0), rows_in[...]))
    queries.start()
    hidden_1.to_z()
    hidden_2.to_z()

    grad_k = jnp.zeros((latents, columns), F32)
    grad_v = jnp.zeros((latents, columns), F32)
    for h in range(heads):
        d_att_h = jnp.where(lane_head == h, d_att, jnp.zeros_like(d_att))
        q_h = jnp.where(lane_head == h, query, jnp.zeros_like(query))
        grad_k += dot(ds_ref[h], q_h)
        grad_v += dot(probs[h], d_att_h)
        if h == 0:
            queries.to_x()
    grads = jnp.concatenate([grad_k, grad_v], axis=1).astype(BF16)
    gkv[...] = grads.reshape(gkv.shape)
    gc_pair, gx_pair, gz_pair, gf_pair = net.pair(), net.pair(), net.pair(), net.pair()
    net.send(gkv.at[other], gkv_cr, gc_pair, net.sibling())
    net.later(gkv_cr, gc_pair)

    block_rows(outs, dot(att_t[...], d_mixed))
    outs.start()
    net.arrived(small_cr, sc_pair[1])
    small_x[x] = small_0[c] + small_cr[...]
    for d in far_first(NX):
        net.send(small_x.at[x], small_x.at[x], sx_pair, net.x_at(d))
    net.later(small_x.at[pl.ds(0, NX - 1)], sx_pair)

    net.arrived(gkv_cr, gc_pair[1])
    gkv_xs[...] = (gkv[c].astype(F32) + gkv_cr[...].astype(F32)).astype(BF16)
    for d in far_first(NX):
        net.send(gkv_xs.at[(x + d) % NX], gkv_xr.at[d - 1], gx_pair, net.x_at(d))
    net.later(gkv_xr, gx_pair)

    outs.to_x()
    queries.to_z()
    outs.to_z()
    net.arrived(small_x.at[pl.ds(0, NX - 1)], sx_pair[1])
    line = small_x[0]
    for i in range(1, NX):
        line += small_x[i]
    small_z[z] = line
    for d in far_first(nz):
        net.send(small_z.at[z], small_z.at[z], sz_pair, net.z_at(d))
    net.later(small_z.at[pl.ds(0, nz - 1)], sz_pair)

    total = gkv_xs[x].astype(F32)
    net.arrived(gkv_xr, gx_pair[1])
    for d in range(1, NX):
        total += gkv_xr[d - 1].astype(F32)
    gkv_zs[...] = total.astype(BF16)
    for d in far_first(nz):
        target = (z + d) % nz

        @pl.when(target % 2 == c)
        def _(d=d, target=target):
            net.send(gkv_zs.at[target // 2], gkv_zr.at[d - 1], gz_pair, net.at(z=target))

    @net.ends.append
    def _():
        @pl.when(hub)
        def _():
            net.sent(gkv_zs.at[pl.ds(0, half_z - 1)], gz_pair)

        @pl.when(jnp.logical_not(hub))
        def _():
            net.sent(gkv_zs, gz_pair)

    hidden_1.back_z()
    hidden_2.back_z()
    outs.back_z()
    queries.back_z()

    hidden_1.back_x()
    hidden_2.back_x()

    net.arrived(small_z.at[pl.ds(0, nz - 1)], sz_pair[1])
    line = small_z[0]
    for i in range(1, nz):
        line += small_z[i]
    small_ref[c] = line
    net.send(small_ref.at[c], small_ref.at[c], sf_pair, net.sibling())
    net.later(small_cr, sf_pair)

    @pl.when(hub)
    def _():
        net.arrived(gkv_zr, gz_pair[1])
        total = gkv_zs[z // 2].astype(F32)
        for d in range(1, nz):
            total += gkv_zr[d - 1].astype(F32)
        gkv_sum[...] = total.reshape(gkv_sum.shape)
        net.send(gkv_sum.at[other], okv_ref, gf_pair, net.sibling())
        okv_ref[...] = gkv_sum[c]

    @net.ends.append
    def _():
        @pl.when(hub)
        def _():
            net.sent(gkv_sum.at[other], gf_pair)

    outs.back_x()
    queries.back_x()
    for chunk in sums:
        chunk.back_core()

    @pl.when(jnp.logical_not(hub))
    def _():
        net.arrived(okv_ref, gf_pair[1])

    net.arrived(small_ref.at[other], sf_pair[1])
    stores = [
        pltpu.make_async_copy(okv_ref, okv_hbm, local.at[10]),
        pltpu.make_async_copy(small_ref, small_hbm, local.at[11]),
    ]
    for store in stores:
        store.start()
    for i, chunk in enumerate(sums):
        chunk.end()
        stores.append(pltpu.make_async_copy(ws_full.at[i], ws_hbm.at[i], local.at[12 + i]))
        stores[-1].start()
    for store in stores:
        store.wait()
    net.finish()
    assert net.used <= SEMAPHORES, net.used


def write_kernel(
    ws_hbm,
    small_hbm,
    kv_hbm,
    wq_ref,
    wo_ref,
    wh_ref,
    logit_ref,
    gain_ref,
    keys_ref,
    values_ref,
    ws_ref,
    small_ref,
    kv_ref,
    sems,
):
    loads = [pltpu.make_async_copy(ws_hbm.at[i], ws_ref.at[i], sems.at[i]) for i in range(4)]
    loads.append(pltpu.make_async_copy(small_hbm, small_ref, sems.at[4]))
    loads.append(pltpu.make_async_copy(kv_hbm, kv_ref, sems.at[5]))
    for load in loads:
        load.start()

    def block(i, c, x):
        rows = []
        for r in range(3):
            rows.append(jnp.concatenate([ws_ref[i, c, x, 3 * r + l] for l in range(3)], axis=1))
        return jnp.concatenate(rows, axis=0).astype(F32)

    depth = wh_ref.shape[0] // 2
    for i in range(4):
        loads[i].wait()
        for c in range(NC):
            for x in range(NX):
                if i < 2:
                    row = i * depth + (c * NX + x) * 48
                    wh_ref[row : row + 48, :] = block(i, c, x)
                else:
                    ref = wo_ref if i == 2 else wq_ref
                    ref[x * 48 : x * 48 + 48, c * 384 : c * 384 + 384] = block(i, c, x)
    loads[4].wait()
    lines = [small_ref[i // 5, i % 5] for i in range(9)]
    for i in range(3):
        logit_ref[128 * i : 128 * (i + 1)] = lines[i].reshape(128)
    for i in range(6):
        gain_ref[128 * i : 128 * (i + 1)] = lines[3 + i].reshape(128)
    loads[5].wait()
    columns = keys_ref.shape[1]
    keys_ref[...] = kv_ref[:, :columns]
    values_ref[...] = kv_ref[:, columns:]


def solution(mesh):
    nz = mesh.shape["pts"] // (NX * NC)
    ny = mesh.shape["head"]
    half_z = nz // 2

    def on_device(pool, index, labels, w_query, keys, values, w_out, out_gain, w_hidden, w_logit):
        points, columns = index.shape[0], keys.shape[1]
        width, hidden = w_hidden.shape
        latents = keys.shape[0] * nz * NX * NC
        heads = columns // HD
        vmem = pltpu.VMEM
        tile = (16, 128)
        wide = (16, 2 * columns)
        shapes = [
            jax.ShapeDtypeStruct((4, NC, NX, PIECES) + tile, BF16),
            jax.ShapeDtypeStruct((NC, 5, 1, 128), F32),
            jax.ShapeDtypeStruct((8, 2 * columns), F32),
        ]
        scratch = [vmem(shape.shape, shape.dtype) for shape in shapes] + [
            vmem((columns, pool.shape[0]), BF16),
            vmem((points,), jnp.int32),
            vmem((points,), jnp.int32),
            vmem((width,), BF16),
            vmem((hidden,), BF16),
            vmem((columns, width), BF16),
            vmem(keys.shape, BF16),
            vmem(keys.shape, BF16),
            vmem((ny, points, 128), BF16),
            vmem((ny, points // 2, 128), BF16),
            vmem((points, width), BF16),
            vmem((ny, columns, width), BF16),
            vmem((ny, width, hidden), BF16),
            vmem((ny, 1, hidden), F32),
            vmem((8, 2 * columns), F32),
            vmem((8, 2 * columns), F32),
            vmem((2, NX, half_z) + wide, BF16),
            vmem((points, columns), BF16),
            vmem((heads, latents, points), BF16),
            vmem((columns, points), BF16),
            vmem((ny, heads, points // 2, 128), BF16),
            vmem((2 * columns, latents), BF16),
            vmem((heads, latents, points), BF16),
            vmem((points, width), F32),
            vmem((points, width), BF16),
            vmem((ny, points, hidden), BF16),
            vmem((ny, points, hidden), F32),
            vmem((ny, points, hidden), BF16),
            vmem((4, NC, NX, PIECES) + tile, BF16),
            vmem((4, NX, PIECES) + tile, BF16),
            vmem((4, NX, PIECES) + tile, BF16),
            vmem((4, NX - 1, PIECES) + tile, BF16),
            vmem((4, PIECES) + tile, BF16),
            vmem((4, nz - 1) + tile, BF16),
            vmem((2, NX, half_z) + wide, BF16),
            vmem((NX, half_z) + wide, BF16),
            vmem((NX, half_z) + wide, BF16),
            vmem((NX - 1, half_z) + wide, BF16),
            vmem((half_z,) + wide, BF16),
            vmem((nz - 1,) + wide, BF16),
            vmem((2, 8, 2 * columns), F32),
            vmem((NC, 5, 1, 128), F32),
            vmem((5, 1, 128), F32),
            vmem((NX, 5, 1, 128), F32),
            vmem((nz, 5, 1, 128), F32),
            pltpu.SemaphoreType.DMA((16,)),
            pltpu.SemaphoreType.DMA((SEMAPHORES,)),
        ]
        whole = pl.BlockSpec(memory_space=pltpu.VMEM)
        sums = pl.pallas_call(
            lambda *refs: kernel(nz, ny, *refs),
            out_shape=shapes,
            in_specs=[pl.BlockSpec(memory_space=pl.ANY)] * 10,
            out_specs=[pl.BlockSpec(memory_space=pl.ANY)] * 3,
            scratch_shapes=scratch,
            compiler_params=pltpu.CompilerParams(
                collective_id=0, has_side_effects=True, vmem_limit_bytes=56 * 1024 * 1024
            ),
        )(pool.T, index, labels, out_gain, w_logit, w_query.T, keys, values, w_out, w_hidden)
        outs = pl.pallas_call(
            write_kernel,
            out_shape=[
                jax.ShapeDtypeStruct((columns, width), F32),
                jax.ShapeDtypeStruct((columns, width), F32),
                jax.ShapeDtypeStruct((width, hidden), F32),
                jax.ShapeDtypeStruct((hidden,), F32),
                jax.ShapeDtypeStruct((width,), F32),
                jax.ShapeDtypeStruct(keys.shape, F32),
                jax.ShapeDtypeStruct(keys.shape, F32),
            ],
            in_specs=[pl.BlockSpec(memory_space=pltpu.HBM)] * 3,
            out_specs=[whole] * 7,
            scratch_shapes=[vmem(shape.shape, shape.dtype) for shape in shapes]
            + [pltpu.SemaphoreType.DMA((6,))],
            compiler_params=pltpu.CompilerParams(vmem_limit_bytes=60 * 1024 * 1024),
        )(*sums)
        return (outs[0].T,) + tuple(outs[1:])

    return jax.shard_map(
        on_device,
        mesh=mesh,
        in_specs=(
            P("pts", "head"),
            P("pts"),
            P("pts"),
            P(None, "head"),
            P("pts", "head"),
            P("pts", "head"),
            P("head", None),
            P(),
            P(None, "head"),
            P("head"),
        ),
        out_specs=(
            P(None, "head"),
            P("head", None),
            P(None, "head"),
            P("head"),
            P(),
            P("pts", "head"),
            P("pts", "head"),
        ),
        check_vma=False,
    )
```

time: 119 us -> 96.6 us (0.81)
  local copies, waits for them, and re-layouts: 9.06 us -> 0 us
  Pallas kernels: 104 us -> 95.8 us
  other arithmetic: 5.33 us -> 0 us
    pallas_call x1, Pallas kernels: 104 us -> 93 us  [on_device(): pl.pallas_call(lambda *refs: kernel(nz, ny, *refs), out_shape=shapes, in_...]
    convert_element_type x4 -> x0, other arithmetic: 4.58 us -> none  [the longest x1 2.2 us: on_device(): grad_wh.astype(F32)]
    unnamed x18 -> x0, local copies, waits for them, and re-layouts: 3.76 us -> none
    pallas_call x0 -> x1, Pallas kernels: none -> 2.74 us  [on_device(): pl.pallas_call(write_kernel, out_shape=[jax.ShapeDtypeStruct((columns, wi...]
    reshape x5 -> x0, local copies, waits for them, and re-layouts: 2.68 us -> none  [the longest x1 0.77 us: on_device(): labels.reshape(points, 1)]
    slice x3 -> x0, local copies, waits for them, and re-layouts: 2.62 us -> none  [the longest x1 1.44 us: on_device(): grad_kv[:, columns:]]
where the time goes in v2:
time: 96.6 us; the launch traced here: 96.4 us
  Pallas kernels  95.8 us (99%)
    pallas_call x1, Pallas kernels, on_device(): pl.pallas_call(lambda *refs: kernel(nz, ny, *refs), out_shape=shapes, in_...  93 us
    pallas_call x1, Pallas kernels, on_device(): pl.pallas_call(write_kernel, out_shape=[jax.ShapeDtypeStruct((columns, wi...  2.74 us

profile of v2, /device:TPU:1, one launch (start us, length us, event | category | flops | bytes accessed | tf_op | source)
XLA Modules:
  0.0 96.4 jit_solution(8467587365517000134)
XLA Ops:
  0.6 93.0 %shard_map.153 = (bf16[4,2,4,9,16,128]{5,4,3,2,1,0:T(8,128)(2,1)}, f32[2,5,1,128]{3,2,1,0:T(1,128)}, f32[8,384]{1,0:T(8,128)}) custom-call(bf16[192,576]{1,0:T(8,128)(2,1)} %bitcast.4, s32[288]{0:T(512)} %refs_1_.1, s32[288]{0:T(512)} %refs_2_.1, bf16[768]{0:T(1024)(128)(2,1)} %refs_3_.1, bf16[384]{0:T(512)(128)(2,1)} %refs_4_.1, bf16[192,768]{1,0:T(8,128)(2,1)} %bitcast.3, ...), custom_call_target="tpu_custom_call" | custom-call | tf_op jit(solution)/shard_map/pallas_call | solution.py:836
  93.7 2.7 %shard_map.154 = (f32[192,768]{1,0:T(8,128)}, f32[192,768]{1,0:T(8,128)}, f32[768,384]{1,0:T(8,128)}, f32[384]{0:T(512)}, f32[768]{0:T(1024)}, /*index=5*/f32[8,192]{1,0:T(8,128)}, f32[8,192]{1,0:T(8,128)}) custom-call(bf16[4,2,4,9,16,128]{5,4,3,2,1,0:T(8,128)(2,1)} %get-tuple-element.17.ws_hbm, f32[2,5,1,128]{3,2,1,0:T(1,128)} %get-tuple-element.18.small_hbm, ...), custom_call_target="tpu_custom_call" | custom-call | tf_op jit(solution)/shard_map/pallas_call | solution.py:846

commit v3 on v2

--- a/solution.py
+++ b/solution.py
@@ -9,8 +9,7 @@
 EPSILON = 1e-05
 NX = 4
 NC = 2
-PIECES = 9
-SEMAPHORES = 112
+SEMAPHORES = 96
 MESH = pl.DeviceIdType.MESH
 F32 = jnp.float32
 BF16 = jnp.bfloat16
@@ -115,7 +114,7 @@
     def __init__(self, net, refs, mirrored):
         self.net, self.mirrored = net, mirrored
         self.part, self.cr, self.xs, self.xr, self.zs, self.zr, self.full = refs
-        nz = net.nz
+        self.count = self.zs.shape[0]
         self.core, self.x, self.z = net.pair(), net.pair(), net.pair()
         self.gz, self.gx, self.gc = net.pair(), net.pair(), net.pair()
         self.piece, self.reduces = self.role(net.z)
@@ -123,18 +122,14 @@
     def role(self, z):
         nz = self.net.nz
         spot = (nz - 1 - z) if self.mirrored else z
-        piece = (PIECES * spot + nz - 1) // nz
-        return jnp.minimum(piece, PIECES - 1), (nz * piece) // PIECES == spot
-
-    def owner(self, piece):
-        spot = (self.net.nz * piece) // PIECES
-        return self.net.nz - 1 - spot if self.mirrored else spot
-
-    def put(self, c, x, block):
+        piece = (self.count * spot + nz - 1) // nz
+        return jnp.minimum(piece, self.count - 1), (nz * piece) // self.count == spot
+
+    def put(self, c, x, block, slot=0):
         block = block.astype(BF16)
-        for j in range(PIECES):
+        for j in range(9):
             r, l = 16 * (j // 3), 128 * (j % 3)
-            self.part[c, x, j] = block[r : r + 16, l : l + 128]
+            self.part[c, x, j, 16 * slot : 16 * slot + 16] = block[r : r + 16, l : l + 128]
 
     def start(self):
         net = self.net
@@ -172,7 +167,7 @@
     def pieces(self, wait):
         @pl.when(self.reduces)
         def _():
-            wait(self.zs.at[pl.ds(0, PIECES - 1)])
+            wait(self.zs.at[pl.ds(0, self.count - 1)])
 
         @pl.when(jnp.logical_not(self.reduces))
         def _():
@@ -231,11 +226,13 @@
     values_hbm,
     w_out_hbm,
     w_hidden_hbm,
-    ws_hbm,
-    small_hbm,
+    hid_hbm,
+    out_hbm,
+    que_hbm,
     okv_hbm,
-    ws_full,
-    small_ref,
+    hid_full,
+    out_full,
+    que_full,
     okv_ref,
     pool,
     index,
@@ -265,12 +262,24 @@
     act_ref,
     slope_ref,
     dh_ref,
-    ws_part,
-    ws_cr,
-    ws_xs,
-    ws_xr,
-    ws_zs,
-    ws_zr,
+    hid_part,
+    hid_cr,
+    hid_xs,
+    hid_xr,
+    hid_zs,
+    hid_zr,
+    out_part,
+    out_cr,
+    out_xs,
+    out_xr,
+    out_zs,
+    out_zr,
+    que_part,
+    que_cr,
+    que_xs,
+    que_xr,
+    que_zs,
+    que_zr,
     gkv,
     gkv_cr,
     gkv_xs,
@@ -278,10 +287,6 @@
     gkv_zs,
     gkv_zr,
     gkv_sum,
-    small_0,
-    small_cr,
-    small_x,
-    small_z,
     local,
     sems,
 ):
@@ -441,6 +446,17 @@
         block = kv_buf.at[c, (x + NX - d) % NX]
         net.send(block, block, kc_pair, net.sibling())
     net.later(gkv_xs, kc_pair)
+    far_y = (y + ny - far) % ny
+    net.arrived(wo_bytes(ny - 1), wo_pair[1])
+    for d in range(1, ny):
+        block = wo_half((y + ny - d) % ny, c)
+        net.send(block, block, fo_pair, net.sibling())
+    net.later(wo_bytes(ny - 1), fo_pair)
+    net.arrived(wh_part(0, 0, 0), far_pair[1])
+    for d in far_first(NX):
+        net.send(wh_part(far_y, c, x), wh_part(far_y, c, x), wx_pair, net.x_at(d))
+    three = wh_full.at[0, pl.ds(0, (NX - 1) * x_rows)]
+    net.later(three, wx_pair)
     net.arrived(gkv_xs, kc_pair[1])
 
     columns = w_query.shape[0]
@@ -468,17 +484,6 @@
             net.send(att_buf.at[y, h], att_buf.at[y, h], att_pair, net.y_at(d))
 
     net.later(att_buf.at[others], att_pair)
-    far_y = (y + ny - far) % ny
-    net.arrived(wo_bytes(ny - 1), wo_pair[1])
-    for d in range(1, ny):
-        block = wo_half((y + ny - d) % ny, c)
-        net.send(block, block, fo_pair, net.sibling())
-    net.later(wo_bytes(ny - 1), fo_pair)
-    net.arrived(wh_part(0, 0, 0), far_pair[1])
-    for d in far_first(NX):
-        net.send(wh_part(far_y, c, x), wh_part(far_y, c, x), wx_pair, net.x_at(d))
-    three = wh_full.at[0, pl.ds(0, (NX - 1) * x_rows)]
-    net.later(three, wx_pair)
     net.arrived(wl_full.at[others], wl_pair[1])
     net.arrived(wh_bytes(ny - 2), near_pair[1])
     for d in range(1, ny):
@@ -512,10 +517,12 @@
     logit = jnp.zeros((points, 1), F32)
     for i in range(ny):
         v = dot(normed_ref[...], wh_full[i])
-        t = jnp.tanh(root * (v + cubic * (v * v * v)))
-        act = (0.5 * v * (1.0 + t)).astype(BF16)
+        v2 = v * v
+        gate = 0.5 + 0.5 * jnp.tanh(v * (root + (root * cubic) * v2))
+        smooth = v * gate
+        act = smooth.astype(BF16)
         act_ref[i] = act
-        slope_ref[i] = 0.5 * (1.0 + t) + 0.5 * v * (1.0 - t * t) * (root * (1.0 + 3.0 * cubic * (v * v)))
+        slope_ref[i] = gate + smooth * (1.0 - gate) * (2.0 * root + (6.0 * root * cubic) * v2)
         logit += jnp.sum(act.astype(F32) * wl_full[i], axis=1, keepdims=True)
     total_points = points * nz * NX * NC
     loads[7].wait()
@@ -525,21 +532,20 @@
     for i in range(ny):
         dh_ref[i] = (d_logit * wl_full[i] * slope_ref[i]).astype(BF16)
 
-    sums = []
-    for i in range(4):
-        refs = [r.at[i] for r in (ws_part, ws_cr, ws_xs, ws_xr, ws_zs, ws_zr, ws_full)]
-        sums.append(WeightSum(net, refs, i % 2 == 1))
-    hidden_1, hidden_2, outs, queries = sums
+    hidden_sum = WeightSum(net, (hid_part, hid_cr, hid_xs, hid_xr, hid_zs, hid_zr, hid_full), False)
+    out_sum = WeightSum(net, (out_part, out_cr, out_xs, out_xr, out_zs, out_zr, out_full), True)
+    query_sum = WeightSum(net, (que_part, que_cr, que_xs, que_xr, que_zs, que_zr, que_full), False)
+    sums = (hidden_sum, out_sum, query_sum)
 
     normed_t = normed_ref[...].T
     depth = normed_t.shape[0] // 2
-    for k, chunk in enumerate((hidden_1, hidden_2)):
+    for k in range(2):
         grad = dot(normed_t[k * depth : (k + 1) * depth], dh_ref[y])
         for cc in range(NC):
             for xx in range(NX):
                 row = (cc * NX + xx) * 48
-                chunk.put(cc, xx, grad[row : row + 48])
-        chunk.start()
+                hidden_sum.put(cc, xx, grad[row : row + 48], k)
+    hidden_sum.start()
     grad_logit = jnp.sum(d_logit * act_ref[y].astype(F32), axis=0, keepdims=True)
 
     d_normed = dot_nt(dh_ref[0], wh_full[0])
@@ -556,23 +562,22 @@
     )
     d_mixed = d_mixed.astype(BF16)
 
-    hidden_1.to_x()
-    hidden_2.to_x()
+    hidden_sum.to_x()
 
     lines = [grad_logit[:, 128 * i : 128 * (i + 1)] for i in range(3)]
     lines += [grad_gain[:, 128 * i : 128 * (i + 1)] for i in range(6)]
-    lines += [jnp.zeros((1, 128), F32)]
-    for i, line in enumerate(lines):
-        small_0[i // 5, i % 5] = line
-    sc_pair, sx_pair, sz_pair, sf_pair = net.pair(), net.pair(), net.pair(), net.pair()
-    net.send(small_0.at[other], small_cr, sc_pair, net.sibling())
-    net.later(small_cr, sc_pair)
+    for i in range(NC * NX):
+        second = lines[8] if i == 0 else jnp.zeros((1, 128), F32)
+        block = jnp.concatenate([lines[i], second, jnp.zeros((14, 128), F32)], axis=0)
+        que_part[i // NX, i % NX, 9] = block.astype(BF16)
 
     def block_rows(chunk, grad):
         for cc in range(NC):
             for xx in range(NX):
                 chunk.put(cc, xx, grad[xx * 48 : xx * 48 + 48, cc * 384 : cc * 384 + 384])
 
+    block_rows(out_sum, dot(att_t[...], d_mixed))
+    out_sum.start()
     w_out = wo_full[y]
     d_att = dot_nt(d_mixed, w_out).astype(BF16)
     d_att_t = dot_nt(w_out, d_mixed).astype(BF16)
@@ -588,10 +593,11 @@
         d_scores = (probs[h].astype(F32) * (d_probs - delta) * scale).astype(BF16)
         ds_ref[h] = d_scores
         d_query.append(dot(kv_t_ref[rows], d_scores).astype(BF16))
-    block_rows(queries, dot(jnp.concatenate(d_query, axis=0), rows_in[...]))
-    queries.start()
-    hidden_1.to_z()
-    hidden_2.to_z()
+        if h == 0:
+            out_sum.to_x()
+    block_rows(query_sum, dot(jnp.concatenate(d_query, axis=0), rows_in[...]))
+    query_sum.start()
+    hidden_sum.to_z()
 
     grad_k = jnp.zeros((latents, columns), F32)
     grad_v = jnp.zeros((latents, columns), F32)
@@ -601,38 +607,24 @@
         grad_k += dot(ds_ref[h], q_h)
         grad_v += dot(probs[h], d_att_h)
         if h == 0:
-            queries.to_x()
+            query_sum.to_x()
+            out_sum.to_z()
     grads = jnp.concatenate([grad_k, grad_v], axis=1).astype(BF16)
     gkv[...] = grads.reshape(gkv.shape)
     gc_pair, gx_pair, gz_pair, gf_pair = net.pair(), net.pair(), net.pair(), net.pair()
     net.send(gkv.at[other], gkv_cr, gc_pair, net.sibling())
     net.later(gkv_cr, gc_pair)
 
-    block_rows(outs, dot(att_t[...], d_mixed))
-    outs.start()
-    net.arrived(small_cr, sc_pair[1])
-    small_x[x] = small_0[c] + small_cr[...]
-    for d in far_first(NX):
-        net.send(small_x.at[x], small_x.at[x], sx_pair, net.x_at(d))
-    net.later(small_x.at[pl.ds(0, NX - 1)], sx_pair)
-
     net.arrived(gkv_cr, gc_pair[1])
     gkv_xs[...] = (gkv[c].astype(F32) + gkv_cr[...].astype(F32)).astype(BF16)
     for d in far_first(NX):
         net.send(gkv_xs.at[(x + d) % NX], gkv_xr.at[d - 1], gx_pair, net.x_at(d))
     net.later(gkv_xr, gx_pair)
 
-    outs.to_x()
-    queries.to_z()
-    outs.to_z()
-    net.arrived(small_x.at[pl.ds(0, NX - 1)], sx_pair[1])
-    line = small_x[0]
-    for i in range(1, NX):
-        line += small_x[i]
-    small_z[z] = line
-    for d in far_first(nz):
-        net.send(small_z.at[z], small_z.at[z], sz_pair, net.z_at(d))
-    net.later(small_z.at[pl.ds(0, nz - 1)], sz_pair)
+    query_sum.to_z()
+    hidden_sum.back_z()
+    out_sum.back_z()
+    query_sum.back_z()
 
     total = gkv_xs[x].astype(F32)
     net.arrived(gkv_xr, gx_pair[1])
@@ -656,21 +648,9 @@
         def _():
             net.sent(gkv_zs, gz_pair)
 
-    hidden_1.back_z()
-    hidden_2.back_z()
-    outs.back_z()
-    queries.back_z()
-
-    hidden_1.back_x()
-    hidden_2.back_x()
-
-    net.arrived(small_z.at[pl.ds(0, nz - 1)], sz_pair[1])
-    line = small_z[0]
-    for i in range(1, nz):
-        line += small_z[i]
-    small_ref[c] = line
-    net.send(small_ref.at[c], small_ref.at[c], sf_pair, net.sibling())
-    net.later(small_cr, sf_pair)
+    hidden_sum.back_x()
+    out_sum.back_x()
+    query_sum.back_x()
 
     @pl.when(hub)
     def _():
@@ -688,8 +668,6 @@
         def _():
             net.sent(gkv_sum.at[other], gf_pair)
 
-    outs.back_x()
-    queries.back_x()
     for chunk in sums:
         chunk.back_core()
 
@@ -697,16 +675,12 @@
     def _():
         net.arrived(okv_ref, gf_pair[1])
 
-    net.arrived(small_ref.at[other], sf_pair[1])
-    stores = [
-        pltpu.make_async_copy(okv_ref, okv_hbm, local.at[10]),
-        pltpu.make_async_copy(small_ref, small_hbm, local.at[11]),
-    ]
-    for store in stores:
-        store.start()
-    for i, chunk in enumerate(sums):
+    stores = [pltpu.make_async_copy(okv_ref, okv_hbm, local.at[10])]
+    stores[0].start()
+    places = ((hid_full, hid_hbm), (out_full, out_hbm), (que_full, que_hbm))
+    for i, (chunk, (held, target)) in enumerate(zip(sums, places)):
         chunk.end()
-        stores.append(pltpu.make_async_copy(ws_full.at[i], ws_hbm.at[i], local.at[12 + i]))
+        stores.append(pltpu.make_async_copy(held, target, local.at[11 + i]))
         stores[-1].start()
     for store in stores:
         store.wait()
@@ -715,8 +689,9 @@
 
 
 def write_kernel(
-    ws_hbm,
-    small_hbm,
+    hid_hbm,
+    out_hbm,
+    que_hbm,
     kv_hbm,
     wq_ref,
     wo_ref,
@@ -725,41 +700,42 @@
     gain_ref,
     keys_ref,
     values_ref,
-    ws_ref,
-    small_ref,
+    hid_ref,
+    out_ref,
+    que_ref,
     kv_ref,
     sems,
 ):
-    loads = [pltpu.make_async_copy(ws_hbm.at[i], ws_ref.at[i], sems.at[i]) for i in range(4)]
-    loads.append(pltpu.make_async_copy(small_hbm, small_ref, sems.at[4]))
-    loads.append(pltpu.make_async_copy(kv_hbm, kv_ref, sems.at[5]))
+    pairs = ((hid_hbm, hid_ref), (out_hbm, out_ref), (que_hbm, que_ref), (kv_hbm, kv_ref))
+    loads = [pltpu.make_async_copy(a, b, sems.at[i]) for i, (a, b) in enumerate(pairs)]
     for load in loads:
         load.start()
 
-    def block(i, c, x):
+    def block(ref, c, x, slot=0):
         rows = []
         for r in range(3):
-            rows.append(jnp.concatenate([ws_ref[i, c, x, 3 * r + l] for l in range(3)], axis=1))
+            tiles = [ref[c, x, 3 * r + l, 16 * slot : 16 * slot + 16] for l in range(3)]
+            rows.append(jnp.concatenate(tiles, axis=1))
         return jnp.concatenate(rows, axis=0).astype(F32)
 
     depth = wh_ref.shape[0] // 2
-    for i in range(4):
-        loads[i].wait()
-        for c in range(NC):
-            for x in range(NX):
-                if i < 2:
-                    row = i * depth + (c * NX + x) * 48
-                    wh_ref[row : row + 48, :] = block(i, c, x)
-                else:
-                    ref = wo_ref if i == 2 else wq_ref
-                    ref[x * 48 : x * 48 + 48, c * 384 : c * 384 + 384] = block(i, c, x)
-    loads[4].wait()
-    lines = [small_ref[i // 5, i % 5] for i in range(9)]
+    parts = [(c, x) for c in range(NC) for x in range(NX)]
+    loads[0].wait()
+    for slot in range(2):
+        for c, x in parts:
+            row = slot * depth + (c * NX + x) * 48
+            wh_ref[row : row + 48, :] = block(hid_ref, c, x, slot)
+    for load, source, target in ((loads[1], out_ref, wo_ref), (loads[2], que_ref, wq_ref)):
+        load.wait()
+        for c, x in parts:
+            target[x * 48 : x * 48 + 48, c * 384 : c * 384 + 384] = block(source, c, x)
+    vectors = [que_ref[c, x, 9].astype(F32) for c, x in parts]
+    lines = [vector[0:1] for vector in vectors] + [vectors[0][1:2]]
     for i in range(3):
         logit_ref[128 * i : 128 * (i + 1)] = lines[i].reshape(128)
     for i in range(6):
         gain_ref[128 * i : 128 * (i + 1)] = lines[3 + i].reshape(128)
-    loads[5].wait()
+    loads[3].wait()
     columns = keys_ref.shape[1]
     keys_ref[...] = kv_ref[:, :columns]
     values_ref[...] = kv_ref[:, columns:]
@@ -776,13 +752,21 @@
         latents = keys.shape[0] * nz * NX * NC
         heads = columns // HD
         vmem = pltpu.VMEM
-        tile = (16, 128)
         wide = (16, 2 * columns)
+        forms = ((9, (32, 128)), (9, (16, 128)), (10, (16, 128)))
         shapes = [
-            jax.ShapeDtypeStruct((4, NC, NX, PIECES) + tile, BF16),
-            jax.ShapeDtypeStruct((NC, 5, 1, 128), F32),
-            jax.ShapeDtypeStruct((8, 2 * columns), F32),
-        ]
+            jax.ShapeDtypeStruct((NC, NX, count) + tile, BF16) for count, tile in forms
+        ] + [jax.ShapeDtypeStruct((8, 2 * columns), F32)]
+        buffers = []
+        for count, tile in forms:
+            buffers += [
+                vmem((NC, NX, count) + tile, BF16),
+                vmem((NX, count) + tile, BF16),
+                vmem((NX, count) + tile, BF16),
+                vmem((NX - 1, count) + tile, BF16),
+                vmem((count,) + tile, BF16),
+                vmem((nz - 1,) + tile, BF16),
+            ]
         scratch = [vmem(shape.shape, shape.dtype) for shape in shapes] + [
             vmem((columns, pool.shape[0]), BF16),
             vmem((points,), jnp.int32),
@@ -812,12 +796,7 @@
             vmem((ny, points, hidden), BF16),
             vmem((ny, points, hidden), F32),
             vmem((ny, points, hidden), BF16),
-            vmem((4, NC, NX, PIECES) + tile, BF16),
-            vmem((4, NX, PIECES) + tile, BF16),
-            vmem((4, NX, PIECES) + tile, BF16),
-            vmem((4, NX - 1, PIECES) + tile, BF16),
-            vmem((4, PIECES) + tile, BF16),
-            vmem((4, nz - 1) + tile, BF16),
+            *buffers,
             vmem((2, NX, half_z) + wide, BF16),
             vmem((NX, half_z) + wide, BF16),
             vmem((NX, half_z) + wide, BF16),
@@ -825,10 +804,6 @@
             vmem((half_z,) + wide, BF16),
             vmem((nz - 1,) + wide, BF16),
             vmem((2, 8, 2 * columns), F32),
-            vmem((NC, 5, 1, 128), F32),
-            vmem((5, 1, 128), F32),
-            vmem((NX, 5, 1, 128), F32),
-            vmem((nz, 5, 1, 128), F32),
             pltpu.SemaphoreType.DMA((16,)),
             pltpu.SemaphoreType.DMA((SEMAPHORES,)),
         ]
@@ -837,7 +812,7 @@
             lambda *refs: kernel(nz, ny, *refs),
             out_shape=shapes,
             in_specs=[pl.BlockSpec(memory_space=pl.ANY)] * 10,
-            out_specs=[pl.BlockSpec(memory_space=pl.ANY)] * 3,
+            out_specs=[pl.BlockSpec(memory_space=pl.ANY)] * 4,
             scratch_shapes=scratch,
             compiler_params=pltpu.CompilerParams(
                 collective_id=0, has_side_effects=True, vmem_limit_bytes=56 * 1024 * 1024
@@ -854,10 +829,10 @@
                 jax.ShapeDtypeStruct(keys.shape, F32),
                 jax.ShapeDtypeStruct(keys.shape, F32),
             ],
-            in_specs=[pl.BlockSpec(memory_space=pltpu.HBM)] * 3,
+            in_specs=[pl.BlockSpec(memory_space=pltpu.HBM)] * 4,
             out_specs=[whole] * 7,
             scratch_shapes=[vmem(shape.shape, shape.dtype) for shape in shapes]
-            + [pltpu.SemaphoreType.DMA((6,))],
+            + [pltpu.SemaphoreType.DMA((4,))],
             compiler_params=pltpu.CompilerParams(vmem_limit_bytes=60 * 1024 * 1024),
         )(*sums)
         return (outs[0].T,) + tuple(outs[1:])

time: 96.6 us -> 88.6 us (0.917)
  Pallas kernels: 95.8 us -> 87.8 us
    pallas_call x1, Pallas kernels: 93 us -> 85.1 us  [on_device(): pl.pallas_call(lambda *refs: kernel(nz, ny, *refs), out_shape=shapes, in_...]
where the time goes in v3:
time: 88.6 us; the launch traced here: 88.5 us
  Pallas kernels  87.8 us (99%)
    pallas_call x1, Pallas kernels, on_device(): pl.pallas_call(lambda *refs: kernel(nz, ny, *refs), out_shape=shapes, in_...  85.1 us
    pallas_call x1, Pallas kernels, on_device(): pl.pallas_call(write_kernel, out_shape=[jax.ShapeDtypeStruct((columns, wi...  2.73 us

profile of v3, /device:TPU:1, one launch (start us, length us, event | category | flops | bytes accessed | tf_op | source)
XLA Modules:
  0.0 88.5 jit_solution(10797517795965407957)
XLA Ops:
  0.6 85.1 %shard_map.153 = (bf16[2,4,9,32,128]{4,3,2,1,0:T(8,128)(2,1)}, bf16[2,4,9,16,128]{4,3,2,1,0:T(8,128)(2,1)}, bf16[2,4,10,16,128]{4,3,2,1,0:T(8,128)(2,1)}, f32[8,384]{1,0:T(8,128)}) custom-call(bf16[192,576]{1,0:T(8,128)(2,1)} %bitcast.4, s32[288]{0:T(512)} %refs_1_.1, s32[288]{0:T(512)} %refs_2_.1, bf16[768]{0:T(1024)(128)(2,1)} %refs_3_.1, ...), custom_call_target="tpu_custom_call" | custom-call | tf_op jit(solution)/shard_map/pallas_call | solution.py:811
  85.7 2.7 %shard_map.154 = (f32[192,768]{1,0:T(8,128)}, f32[192,768]{1,0:T(8,128)}, f32[768,384]{1,0:T(8,128)}, f32[384]{0:T(512)}, f32[768]{0:T(1024)}, /*index=5*/f32[8,192]{1,0:T(8,128)}, f32[8,192]{1,0:T(8,128)}) custom-call(bf16[2,4,9,32,128]{4,3,2,1,0:T(8,128)(2,1)} %get-tuple-element.18.hid_hbm, bf16[2,4,9,16,128]{4,3,2,1,0:T(8,128)(2,1)} %get-tuple-element.19.out_hbm, ...), custom_call_target="tpu_custom_call" | custom-call | tf_op jit(solution)/shard_map/pallas_call | solution.py:821

commit v4 on v3

--- a/solution.py
+++ b/solution.py
@@ -337,23 +337,6 @@
     def _():
         net.send(kv_own, kvx, kvx_pair, net.sibling())
 
-    loads[2].wait()
-    loads[3].wait()
-    spots = lax.broadcasted_iota(jnp.int32, (pool.shape[1], points), 0)
-    chosen = jnp.where(spots == index[...].reshape(1, points), 1.0, 0.0).astype(BF16)
-    picked = dot(pool[...], chosen).T.astype(BF16)
-    wide, narrow = packed(picked)
-    rows_wide[y] = wide
-    rows_narrow[y] = narrow
-
-    wide_pair, narrow_pair = net.pair(), net.pair()
-    for d in far_first(ny):
-        net.send(rows_wide.at[y], rows_wide.at[y], wide_pair, net.y_at(d))
-        net.send(rows_narrow.at[y], rows_narrow.at[y], narrow_pair, net.y_at(d))
-    others = pl.ds(0, ny - 1)
-    net.later(rows_wide.at[others], wide_pair)
-    net.later(rows_narrow.at[others], narrow_pair)
-
     @pl.when(hub)
     def _():
         net.arrived(kvx, kvx_pair[1])
@@ -363,6 +346,23 @@
         kv_buf[c, x, z // 2] = jnp.concatenate([low, high], axis=0).astype(BF16)
         for d in far_first(nz):
             net.send(kv_tile, kv_tile, (s_kz, (r_kz, z // 2)), net.z_at(d))
+
+    loads[2].wait()
+    loads[3].wait()
+    spots = lax.broadcasted_iota(jnp.int32, (pool.shape[1], points), 0)
+    chosen = jnp.where(spots == index[...].reshape(1, points), 1.0, 0.0).astype(BF16)
+    picked = dot(pool[...], chosen).T.astype(BF16)
+    wide, narrow = packed(picked)
+    rows_wide[y] = wide
+    rows_narrow[y] = narrow
+
+    wide_pair, narrow_pair = net.pair(), net.pair()
+    for d in far_first(ny):
+        net.send(rows_wide.at[y], rows_wide.at[y], wide_pair, net.y_at(d))
+        net.send(rows_narrow.at[y], rows_narrow.at[y], narrow_pair, net.y_at(d))
+    others = pl.ds(0, ny - 1)
+    net.later(rows_wide.at[others], wide_pair)
+    net.later(rows_narrow.at[others], narrow_pair)
 
     @net.ends.append
     def _():
@@ -412,24 +412,17 @@
     net.later(wh_bytes(ny - 2), near_pair)
     net.later(wl_full.at[others], wl_pair)
 
-    side = jnp.where(jnp.logical_and(z % 2 == 0, c == 1), half_z - 1, 1)
-    blocks = []
-    for k in range(half_z):
-        away = (k + 1) // 2
-        step = away * side if k % 2 else (half_z - away) * side
-        block = (z // 2 + step) % half_z
-        blocks.append(block)
-        tile = kv_buf.at[c, x, block]
-        if k:
-            net.arrived(tile, (r_kz, block))
-        else:
-
-            @pl.when(jnp.logical_not(hub))
-            def _(tile=tile, block=block):
-                net.arrived(tile, (r_kz, block))
-
-        for d in far_first(NX):
-            net.send(tile, tile, kx_pair, net.x_at(d))
+    for i in range(half_z):
+        tile = kv_buf.at[c, x, i]
+
+        @pl.when(jnp.logical_or(jnp.logical_not(hub), z // 2 != i))
+        def _(tile=tile, i=i):
+            net.arrived(tile, (r_kz, i))
+
+        if i % 2:
+            two = kv_buf.at[c, x, pl.ds(i - 1, 2)]
+            for d in far_first(NX):
+                net.send(two, two, kx_pair, net.x_at(d))
     net.later(gkv_xr, kx_pair)
     net.arrived(rows_wide.at[others], wide_pair[1])
     net.arrived(rows_narrow.at[others], narrow_pair[1])
@@ -463,8 +456,8 @@
     heads = columns // HD
     latents = 16 * half_z * NX * 2
     kv = kv_buf[...].reshape(latents, 2 * columns)
-    kv_t_ref[...] = kv.T
     k_all, v_all = kv[:, :columns], kv[:, columns:]
+    kv_t_ref[columns:] = v_all.T
     att_pair = net.pair()
     lane_head = lax.broadcasted_iota(jnp.int32, (points, columns), 1) // HD
     scale = HD ** (-0.5)
@@ -484,6 +477,7 @@
             net.send(att_buf.at[y, h], att_buf.at[y, h], att_pair, net.y_at(d))
 
     net.later(att_buf.at[others], att_pair)
+    kv_t_ref[:columns] = k_all.T
     net.arrived(wl_full.at[others], wl_pair[1])
     net.arrived(wh_bytes(ny - 2), near_pair[1])
     for d in range(1, ny):
@@ -626,6 +620,7 @@
     out_sum.back_z()
     query_sum.back_z()
 
+    hidden_sum.back_x()
     total = gkv_xs[x].astype(F32)
     net.arrived(gkv_xr, gx_pair[1])
     for d in range(1, NX):
@@ -648,10 +643,11 @@
         def _():
             net.sent(gkv_zs, gz_pair)
 
-    hidden_sum.back_x()
     out_sum.back_x()
     query_sum.back_x()
 
+    hidden_sum.back_core()
+    out_sum.back_core()
     @pl.when(hub)
     def _():
         net.arrived(gkv_zr, gz_pair[1])
@@ -668,8 +664,7 @@
         def _():
             net.sent(gkv_sum.at[other], gf_pair)
 
-    for chunk in sums:
-        chunk.back_core()
+    query_sum.back_core()
 
     @pl.when(jnp.logical_not(hub))
     def _():

time: 88.6 us -> 86.6 us (0.977)
  Pallas kernels: 87.8 us -> 85.8 us
    pallas_call x1, Pallas kernels: 85.1 us -> 83 us  [on_device(): pl.pallas_call(lambda *refs: kernel(nz, ny, *refs), out_shape=shapes, in_...]
where the time goes in v4:
time: 86.6 us; the launch traced here: 86.4 us
  Pallas kernels  85.8 us (99%)
    pallas_call x1, Pallas kernels, on_device(): pl.pallas_call(lambda *refs: kernel(nz, ny, *refs), out_shape=shapes, in_...  83 us
    pallas_call x1, Pallas kernels, on_device(): pl.pallas_call(write_kernel, out_shape=[jax.ShapeDtypeStruct((columns, wi...  2.73 us

profile of v4, /device:TPU:1, one launch (start us, length us, event | category | flops | bytes accessed | tf_op | source)
XLA Modules:
  0.0 86.4 jit_solution(14922433199050784632)
XLA Ops:
  0.6 83.0 %shard_map.153 = (bf16[2,4,9,32,128]{4,3,2,1,0:T(8,128)(2,1)}, bf16[2,4,9,16,128]{4,3,2,1,0:T(8,128)(2,1)}, bf16[2,4,10,16,128]{4,3,2,1,0:T(8,128)(2,1)}, f32[8,384]{1,0:T(8,128)}) custom-call(bf16[192,576]{1,0:T(8,128)(2,1)} %bitcast.4, s32[288]{0:T(512)} %refs_1_.1, s32[288]{0:T(512)} %refs_2_.1, bf16[768]{0:T(1024)(128)(2,1)} %refs_3_.1, ...), custom_call_target="tpu_custom_call" | custom-call | tf_op jit(solution)/shard_map/pallas_call | solution.py:806
  83.7 2.7 %shard_map.154 = (f32[192,768]{1,0:T(8,128)}, f32[192,768]{1,0:T(8,128)}, f32[768,384]{1,0:T(8,128)}, f32[384]{0:T(512)}, f32[768]{0:T(1024)}, /*index=5*/f32[8,192]{1,0:T(8,128)}, f32[8,192]{1,0:T(8,128)}) custom-call(bf16[2,4,9,32,128]{4,3,2,1,0:T(8,128)(2,1)} %get-tuple-element.18.hid_hbm, bf16[2,4,9,16,128]{4,3,2,1,0:T(8,128)(2,1)} %get-tuple-element.19.out_hbm, ...), custom_call_target="tpu_custom_call" | custom-call | tf_op jit(solution)/shard_map/pallas_call | solution.py:816

commit v5 on v4

--- a/solution.py
+++ b/solution.py
@@ -646,8 +646,8 @@
     out_sum.back_x()
     query_sum.back_x()
 
-    hidden_sum.back_core()
-    out_sum.back_core()
+    for chunk in sums:
+        chunk.back_core()
     @pl.when(hub)
     def _():
         net.arrived(gkv_zr, gz_pair[1])
@@ -664,19 +664,19 @@
         def _():
             net.sent(gkv_sum.at[other], gf_pair)
 
-    query_sum.back_core()
-
-    @pl.when(jnp.logical_not(hub))
-    def _():
-        net.arrived(okv_ref, gf_pair[1])
-
-    stores = [pltpu.make_async_copy(okv_ref, okv_hbm, local.at[10])]
-    stores[0].start()
+    stores = []
     places = ((hid_full, hid_hbm), (out_full, out_hbm), (que_full, que_hbm))
     for i, (chunk, (held, target)) in enumerate(zip(sums, places)):
         chunk.end()
         stores.append(pltpu.make_async_copy(held, target, local.at[11 + i]))
         stores[-1].start()
+
+    @pl.when(jnp.logical_not(hub))
+    def _():
+        net.arrived(okv_ref, gf_pair[1])
+
+    stores.append(pltpu.make_async_copy(okv_ref, okv_hbm, local.at[10]))
+    stores[-1].start()
     for store in stores:
         store.wait()
     net.finish()

time: 86.6 us -> 86.6 us (level)
  no operation moved by 1% of the time
where the time goes in v5:
time: 86.6 us; the launch traced here: 86.4 us
  Pallas kernels  85.8 us (99%)
    pallas_call x1, Pallas kernels, on_device(): pl.pallas_call(lambda *refs: kernel(nz, ny, *refs), out_shape=shapes, in_...  83.1 us
    pallas_call x1, Pallas kernels, on_device(): pl.pallas_call(write_kernel, out_shape=[jax.ShapeDtypeStruct((columns, wi...  2.73 us

profile of v5, /device:TPU:1, one launch (start us, length us, event | category | flops | bytes accessed | tf_op | source)
XLA Modules:
  0.0 86.4 jit_solution(6431536781436588640)
XLA Ops:
  0.6 83.1 %shard_map.153 = (bf16[2,4,9,32,128]{4,3,2,1,0:T(8,128)(2,1)}, bf16[2,4,9,16,128]{4,3,2,1,0:T(8,128)(2,1)}, bf16[2,4,10,16,128]{4,3,2,1,0:T(8,128)(2,1)}, f32[8,384]{1,0:T(8,128)}) custom-call(bf16[192,576]{1,0:T(8,128)(2,1)} %bitcast.4, s32[288]{0:T(512)} %refs_1_.1, s32[288]{0:T(512)} %refs_2_.1, bf16[768]{0:T(1024)(128)(2,1)} %refs_3_.1, ...), custom_call_target="tpu_custom_call" | custom-call | tf_op jit(solution)/shard_map/pallas_call | solution.py:806
  83.7 2.7 %shard_map.154 = (f32[192,768]{1,0:T(8,128)}, f32[192,768]{1,0:T(8,128)}, f32[768,384]{1,0:T(8,128)}, f32[384]{0:T(512)}, f32[768]{0:T(1024)}, /*index=5*/f32[8,192]{1,0:T(8,128)}, f32[8,192]{1,0:T(8,128)}) custom-call(bf16[2,4,9,32,128]{4,3,2,1,0:T(8,128)(2,1)} %get-tuple-element.18.hid_hbm, bf16[2,4,9,16,128]{4,3,2,1,0:T(8,128)(2,1)} %get-tuple-element.19.out_hbm, ...), custom_call_target="tpu_custom_call" | custom-call | tf_op jit(solution)/shard_map/pallas_call | solution.py:816
